TPU v7x, 32 devices: a whole 2x2x4 slice. The times are simulated.
32 devices in a mesh: seq: 8 (over z, x), dp: 4 (over y, core).
Axes of the slice: x: 2, y: 2, z: 4, core: 2. Of those that a mesh axis runs over, the one named last changes fastest.
Arguments:
- queries: bfloat16 [4, 2048, 1024], P('dp', 'seq'), may hold values from -8 to 8
- key_rows: bfloat16 [4, 2048, 1024], P('dp', 'seq'), may hold values from -8 to 8
- value_rows: bfloat16 [4, 2048, 1024], P('dp', 'seq'), may hold values from -16 to 16
- conv_key: float32 [3, 4, 1024], replicated, may hold values from -2.5 to 2.5
- conv_value: float32 [3, 4, 1024], replicated, may hold values from -2.5 to 2.5
- grad_out: bfloat16 [4, 2048, 1024], P('dp', 'seq'), may hold values from -12 to 12
Outputs:
- attended: bfloat16 [4, 2048, 1024], P('dp', 'seq')
- grad_query: bfloat16 [4, 2048, 1024], P('dp', 'seq')
- grad_key: bfloat16 [4, 2048, 1024], P('dp', 'seq')
- grad_value: bfloat16 [4, 2048, 1024], P('dp', 'seq')
- grad_conv_key: float32 [3, 4, 1024], replicated
- grad_conv_value: float32 [3, 4, 1024], replicated
All inputs are finite; a program needn't handle non-finite values.
Results may differ from a plain program's by a relative error of at most 0.019.
Values may be sent and summed in bfloat16 or wider, within the bound.
A program may use at most 128 MiB of HBM per device.

v0:
```python
import jax
import jax.numpy as jnp
from jax import lax
from jax.sharding import PartitionSpec as P

HEADS = 8
HEAD_DIM = 128
BLOCK = 128


def passed_along(value, axis, steps):
    count = lax.axis_size(axis)
    initial, last = (max(0, -steps), min(count, count - steps))
    return lax.ppermute(value, axis, [(source, source + steps) for source in range(initial, last)])


def partner_2(array, axis, distance):
    return lax.ppermute(array, axis, [(i, i ^ 1 << distance) for i in range(lax.axis_size(axis))])


def coarsen(extended, weight):
    out_rows = (extended.shape[1] - 2) // 2
    summed = weight[0] * extended[:, 0 : 2 * out_rows : 2].astype(jnp.float32)
    for offset in range(1, 4):
        summed = summed + weight[offset] * extended[:, offset : offset + 2 * out_rows : 2].astype(
            jnp.float32
        )
    return summed.astype(jnp.bfloat16)


def coarsen_back(upstream, extended, weight):
    seqs_dev, out_rows, feat_width = upstream.shape
    zero_row = jnp.zeros((seqs_dev, 1, feat_width), jnp.float32)
    even_rows = jnp.concatenate([weight[0] * upstream, zero_row], 1) + jnp.concatenate(
        [zero_row, weight[2] * upstream], 1
    )
    odd_rows = jnp.concatenate([weight[1] * upstream, zero_row], 1) + jnp.concatenate(
        [zero_row, weight[3] * upstream], 1
    )
    spread = jnp.stack([even_rows, odd_rows], 2).reshape(seqs_dev, 2 * out_rows + 2, feat_width)
    weight_grad = jnp.stack(
        [
            jnp.sum(
                upstream * extended[:, offset : offset + 2 * out_rows : 2].astype(jnp.float32),
                (0, 1),
            )
            for offset in range(4)
        ]
    )
    return (spread, weight_grad)


def move_near(moved_rows, shift_by):
    return passed_along(moved_rows, "seq", shift_by)


def move_grads(moved_rows, shift_by):
    return passed_along(moved_rows.astype(jnp.bfloat16), "seq", shift_by).astype(moved_rows.dtype)


def per_device(queries, key_rows, value_rows, conv_key, conv_value, grad_out):
    seqs_dev, tok_rows, feat_width = queries.shape
    levels = conv_key.shape[0]
    head_count = HEADS
    head_size = HEAD_DIM
    blk_rows = BLOCK
    blocks_here = tok_rows // blk_rows
    local_top = blocks_here.bit_length() - 1
    seq_devices = lax.axis_size("seq")
    dev_index = lax.axis_index("seq")
    total_blocks = blocks_here * seq_devices
    score_scale = head_size ** (-0.5)
    pair_width = 2 * feat_width
    group_heads = 2
    kv_weight = jnp.stack(
        [
            conv_key.reshape(levels, 4, head_count, head_size),
            conv_value.reshape(levels, 4, head_count, head_size),
        ],
        3,
    ).reshape(levels, 4, pair_width)
    fine_pairs = jnp.stack(
        [
            key_rows.reshape(seqs_dev, tok_rows, head_count, head_size),
            value_rows.reshape(seqs_dev, tok_rows, head_count, head_size),
        ],
        3,
    ).reshape(seqs_dev, tok_rows, pair_width)
    own_rows = [fine_pairs]
    left_rims = [move_near(fine_pairs[:, -blk_rows:], 1)]
    right_rims = [move_near(fine_pairs[:, :blk_rows], -1)]
    extended_local = [None]
    level_id = 1
    extended = jnp.concatenate([left_rims[level_id - 1][:, -2:], own_rows[level_id - 1]], 1)
    extended_local.append(extended)
    coarse = coarsen(extended, kv_weight[level_id - 1])
    own_rows.append(coarse)
    left_rims.append(move_near(coarse, 1))
    right_rims.append(move_near(coarse, -1))
    block_now = own_rows[local_top]
    left_now = left_rims[local_top]
    group_lefts, group_rights, group_extended, group_first = ([], [], [], [])
    for level_id in range(local_top + 1, levels + 1):
        swap_bit = level_id - local_top - 1
        extended = jnp.concatenate([left_now[:, -2:], block_now], 1)
        group_extended.append(extended)
        own_half = coarsen(extended, kv_weight[level_id - 1])
        partner = partner_2(own_half, "seq", swap_bit)
        is_first = dev_index // 2**swap_bit % 2 == 0
        group_first.append(is_first)
        block_now = jnp.where(
            is_first,
            jnp.concatenate([own_half, partner], 1),
            jnp.concatenate([partner, own_half], 1),
        )
        stride_dev = 2 ** (level_id - local_top)
        left_now = move_near(block_now, stride_dev)
        right_now = move_near(block_now, -stride_dev)
        group_lefts.append(left_now)
        group_rights.append(right_now)
    glob_blocks = dev_index * blocks_here + jnp.arange(blocks_here, dtype=jnp.int32)
    always = jnp.ones((blocks_here,), jnp.bool_)
    sources = []
    pieces = []
    for level_id in range(local_top + 1):
        block_count = blocks_here >> level_id
        padded = jnp.concatenate([left_rims[level_id], own_rows[level_id], right_rims[level_id]], 1)
        sources.append(
            padded.reshape(seqs_dev, block_count + 2, blk_rows, head_count, 2, head_size)
        )
        coarse_id = glob_blocks // 2**level_id
        spread = 2**level_id
        pieces.append((level_id, 0, spread, coarse_id >= 1))
        if level_id == 0:
            pieces.append((0, 1, 1, always))
        pieces.append((level_id, 2, spread, coarse_id + 1 < total_blocks // 2**level_id))
    for slot_id in range(levels - local_top):
        level_id = local_top + 1 + slot_id
        coarse_id = glob_blocks // 2**level_id
        sources.append(
            group_lefts[slot_id].reshape(seqs_dev, 1, blk_rows, head_count, 2, head_size)
        )
        pieces.append((len(sources) - 1, 0, blocks_here, coarse_id >= 1))
        sources.append(
            group_rights[slot_id].reshape(seqs_dev, 1, blk_rows, head_count, 2, head_size)
        )
        pieces.append(
            (len(sources) - 1, 0, blocks_here, coarse_id + 1 < total_blocks // 2**level_id)
        )
    query_blocks = queries.reshape(seqs_dev, blocks_here, blk_rows, head_count, head_size)
    out_blocks = grad_out.reshape(seqs_dev, blocks_here, blk_rows, head_count, head_size)

    def head_group(group_id, loop_state):
        attended_acc, grad_q_acc, source_grads, log_totals, row_deltas = loop_state
        head_start = group_id * group_heads
        q_part = lax.dynamic_slice_in_dim(query_blocks, head_start, group_heads, 3)
        do_part = lax.dynamic_slice_in_dim(out_blocks, head_start, group_heads, 3)
        source_parts = [
            lax.dynamic_slice_in_dim(source, head_start, group_heads, 3) for source in sources
        ]
        score_list = []
        views = []
        for source_id, offset, spread, valid_mask in pieces:
            block_count = blocks_here // spread
            key_blocks = source_parts[source_id][:, offset : offset + block_count]
            q_view = q_part.reshape(seqs_dev, block_count, spread, blk_rows, group_heads, head_size)
            do_view = do_part.reshape(
                seqs_dev, block_count, spread, blk_rows, group_heads, head_size
            )
            raw_scores = jnp.einsum(
                "bnrqhe,bnkhe->bnrhqk",
                q_view,
                key_blocks[..., 0, :],
                preferred_element_type=jnp.float32,
            )
            raw_scores = (
                raw_scores.reshape(seqs_dev, blocks_here, group_heads, blk_rows, blk_rows)
                * score_scale
            )
            score_list.append(
                jnp.where(valid_mask[None, :, None, None, None], raw_scores, -jnp.inf)
            )
            views.append((key_blocks, q_view, do_view, block_count, spread))
        all_scores = jnp.concatenate(score_list, 4)
        row_max = jnp.max(all_scores, 4, keepdims=True)
        exp_scores = jnp.exp(all_scores - row_max)
        summed = jnp.sum(exp_scores, 4, keepdims=True)
        prob_full = exp_scores / summed
        probs_low = prob_full.astype(jnp.bfloat16)
        attended_part = jnp.zeros(
            (seqs_dev, blocks_here, blk_rows, group_heads, head_size), jnp.float32
        )
        grad_prob_list = []
        for piece_id, (key_blocks, q_view, do_view, block_count, spread) in enumerate(views):
            p_slice = probs_low[..., piece_id * blk_rows : (piece_id + 1) * blk_rows].reshape(
                seqs_dev, block_count, spread, group_heads, blk_rows, blk_rows
            )
            attended_part = attended_part + jnp.einsum(
                "bnrhqk,bnkhe->bnrqhe",
                p_slice,
                key_blocks[..., 1, :],
                preferred_element_type=jnp.float32,
            ).reshape(attended_part.shape)
            grad_prob = jnp.einsum(
                "bnrqhe,bnkhe->bnrhqk",
                do_view,
                key_blocks[..., 1, :],
                preferred_element_type=jnp.float32,
            )
            grad_prob_list.append(
                grad_prob.reshape(seqs_dev, blocks_here, group_heads, blk_rows, blk_rows)
            )
        grad_prob_all = jnp.concatenate(grad_prob_list, 4)
        row_delta = jnp.sum(prob_full * grad_prob_all, 4, keepdims=True)
        dscore = (prob_full * (grad_prob_all - row_delta) * score_scale).astype(jnp.bfloat16)
        grad_q_part = jnp.zeros(
            (seqs_dev, blocks_here, blk_rows, group_heads, head_size), jnp.float32
        )
        group_grads = [jnp.zeros(part_arr.shape, jnp.float32) for part_arr in source_parts]
        for piece_id, (key_blocks, q_view, do_view, block_count, spread) in enumerate(views):
            source_id, offset = (pieces[piece_id][0], pieces[piece_id][1])
            p_slice = probs_low[..., piece_id * blk_rows : (piece_id + 1) * blk_rows].reshape(
                seqs_dev, block_count, spread, group_heads, blk_rows, blk_rows
            )
            ds_slice = dscore[..., piece_id * blk_rows : (piece_id + 1) * blk_rows].reshape(
                seqs_dev, block_count, spread, group_heads, blk_rows, blk_rows
            )
            grad_q_part = grad_q_part + jnp.einsum(
                "bnrhqk,bnkhe->bnrqhe",
                ds_slice,
                key_blocks[..., 0, :],
                preferred_element_type=jnp.float32,
            ).reshape(grad_q_part.shape)
            key_grad = jnp.einsum(
                "bnrhqk,bnrqhe->bnkhe", ds_slice, q_view, preferred_element_type=jnp.float32
            )
            value_grad = jnp.einsum(
                "bnrhqk,bnrqhe->bnkhe", p_slice, do_view, preferred_element_type=jnp.float32
            )
            pair_grad = jnp.stack([key_grad, value_grad], 4)
            group_grads[source_id] = (
                group_grads[source_id].at[:, offset : offset + block_count].add(pair_grad)
            )
        attended_acc = lax.dynamic_update_slice_in_dim(
            attended_acc, attended_part.astype(jnp.bfloat16), head_start, 3
        )
        grad_q_acc = lax.dynamic_update_slice_in_dim(
            grad_q_acc, grad_q_part.astype(jnp.bfloat16), head_start, 3
        )
        source_grads = tuple(
            (
                lax.dynamic_update_slice_in_dim(whole, group_part, head_start, 3)
                for whole, group_part in zip(source_grads, group_grads)
            )
        )
        log_totals = lax.dynamic_update_slice_in_dim(
            log_totals, (row_max + jnp.log(summed))[..., 0], head_start, 2
        )
        row_deltas = lax.dynamic_update_slice_in_dim(row_deltas, row_delta[..., 0], head_start, 2)
        return (attended_acc, grad_q_acc, source_grads, log_totals, row_deltas)

    start_state = (
        jnp.zeros((seqs_dev, blocks_here, blk_rows, head_count, head_size), jnp.bfloat16),
        jnp.zeros((seqs_dev, blocks_here, blk_rows, head_count, head_size), jnp.bfloat16),
        tuple((jnp.zeros(source.shape, jnp.float32) for source in sources)),
        jnp.zeros((seqs_dev, blocks_here, head_count, blk_rows), jnp.float32),
        jnp.zeros((seqs_dev, blocks_here, head_count, blk_rows), jnp.float32),
    )
    attended_acc, grad_q_acc, source_grads, log_totals, row_deltas = lax.fori_loop(
        0, head_count // group_heads, head_group, start_state
    )
    attended = attended_acc.reshape(seqs_dev, tok_rows, feat_width)
    grad_query = grad_q_acc.reshape(seqs_dev, tok_rows, feat_width)
    grad_left, grad_own, grad_right = ([], [], [])
    for level_id in range(local_top + 1):
        flat_grad = source_grads[level_id].reshape(seqs_dev, -1, pair_width)
        grad_left.append(flat_grad[:, :blk_rows])
        grad_own.append(flat_grad[:, blk_rows:-blk_rows])
        grad_right.append(flat_grad[:, -blk_rows:])
    group_left_grads = [
        source_grads[local_top + 1 + 2 * slot_id].reshape(seqs_dev, blk_rows, pair_width)
        for slot_id in range(levels - local_top)
    ]
    group_right_grads = [
        source_grads[local_top + 2 + 2 * slot_id].reshape(seqs_dev, blk_rows, pair_width)
        for slot_id in range(levels - local_top)
    ]
    weight_grads = [None] * levels
    carry_block = jnp.zeros((seqs_dev, blk_rows, pair_width), jnp.float32)
    carry_left = jnp.zeros((seqs_dev, 2, pair_width), jnp.float32)
    for level_id in range(levels, local_top, -1):
        slot_id = level_id - local_top - 1
        stride_dev = 2 ** (level_id - local_top)
        left_total = group_left_grads[slot_id].at[:, -2:].add(carry_left)
        block_total = (
            carry_block
            + move_grads(left_total, -stride_dev)
            + move_grads(group_right_grads[slot_id], stride_dev)
        )
        first_part = block_total[:, : blk_rows // 2]
        second_part = block_total[:, blk_rows // 2 :]
        keep_part = jnp.where(group_first[slot_id], first_part, second_part)
        give_part = jnp.where(group_first[slot_id], second_part, first_part)
        half_grad = keep_part + partner_2(give_part.astype(jnp.bfloat16), "seq", slot_id).astype(
            give_part.dtype
        )
        spread, weight_grads[level_id - 1] = coarsen_back(
            half_grad, group_extended[slot_id], kv_weight[level_id - 1]
        )
        carry_left = spread[:, :2]
        carry_block = spread[:, 2:]
    grad_left[local_top] = grad_left[local_top].at[:, -2:].add(carry_left)
    grad_own[local_top] = grad_own[local_top] + carry_block
    fine_left_conv = jnp.zeros((seqs_dev, blk_rows, pair_width), jnp.float32)
    level_id = 1
    from_right = move_grads(grad_left[level_id], -1)
    from_left = move_grads(grad_right[level_id], 1)
    level_grad = (
        grad_own[level_id].at[:, :blk_rows].add(from_left).at[:, -blk_rows:].add(from_right)
    )
    spread, weight_grads[level_id - 1] = coarsen_back(
        level_grad, extended_local[level_id], kv_weight[level_id - 1]
    )
    fine_left_conv = fine_left_conv.at[:, -2:].add(spread[:, :2])
    grad_own[level_id - 1] = grad_own[level_id - 1] + spread[:, 2:]

    def owner_terms(sent_rows, sent_stats, pair_rows):
        q_rows = sent_rows[:, :, :feat_width].reshape(seqs_dev, blk_rows, head_count, head_size)
        do_rows = sent_rows[:, :, feat_width:].reshape(seqs_dev, blk_rows, head_count, head_size)
        pair_view = pair_rows.reshape(seqs_dev, blk_rows, head_count, 2, head_size)
        raw_scores = (
            jnp.einsum(
                "bqhe,bkhe->bhqk", q_rows, pair_view[..., 0, :], preferred_element_type=jnp.float32
            )
            * score_scale
        )
        prob_full = jnp.exp(raw_scores - sent_stats[:, 0][..., None])
        grad_prob = jnp.einsum(
            "bqhe,bkhe->bhqk", do_rows, pair_view[..., 1, :], preferred_element_type=jnp.float32
        )
        dscore = (prob_full * (grad_prob - sent_stats[:, 1][..., None]) * score_scale).astype(
            jnp.bfloat16
        )
        key_grad = jnp.einsum("bhqk,bqhe->bkhe", dscore, q_rows, preferred_element_type=jnp.float32)
        value_grad = jnp.einsum(
            "bhqk,bqhe->bkhe",
            prob_full.astype(jnp.bfloat16),
            do_rows,
            preferred_element_type=jnp.float32,
        )
        return jnp.stack([key_grad, value_grad], 3).reshape(seqs_dev, blk_rows, pair_width)

    from_right = move_grads(fine_left_conv, -1)
    query_tail = jnp.concatenate([queries[:, -blk_rows:], grad_out[:, -blk_rows:]], 2)
    query_front = jnp.concatenate([queries[:, :blk_rows], grad_out[:, :blk_rows]], 2)
    stats_tail = jnp.stack([log_totals[:, -1], row_deltas[:, -1]], 1)
    stats_front = jnp.stack([log_totals[:, 0], row_deltas[:, 0]], 1)
    tail_from_left = move_near(query_tail, 1)
    front_from_right = move_near(query_front, -1)
    stats_from_left = move_grads(stats_tail, 1)
    stats_from_right = move_grads(stats_front, -1)
    left_terms = owner_terms(tail_from_left, stats_from_left, fine_pairs[:, :blk_rows])
    right_terms = owner_terms(front_from_right, stats_from_right, fine_pairs[:, -blk_rows:])
    fine_grad = (
        grad_own[0].at[:, :blk_rows].add(left_terms).at[:, -blk_rows:].add(right_terms + from_right)
    )
    grad_pairs = fine_grad.reshape(seqs_dev, tok_rows, head_count, 2, head_size)
    grad_key = (
        grad_pairs[:, :, :, 0, :].reshape(seqs_dev, tok_rows, feat_width).astype(jnp.bfloat16)
    )
    grad_value = (
        grad_pairs[:, :, :, 1, :].reshape(seqs_dev, tok_rows, feat_width).astype(jnp.bfloat16)
    )
    weight_sum = lax.psum(jnp.stack(weight_grads), ("seq", "dp")).reshape(
        levels, 4, head_count, 2, head_size
    )
    grad_conv_key = weight_sum[:, :, :, 0, :].reshape(levels, 4, feat_width)
    grad_conv_value = weight_sum[:, :, :, 1, :].reshape(levels, 4, feat_width)
    return (attended, grad_query, grad_key, grad_value, grad_conv_key, grad_conv_value)


def solution(mesh):
    in_specs = (
        P("dp", "seq", None),
        P("dp", "seq", None),
        P("dp", "seq", None),
        P(),
        P(),
        P("dp", "seq", None),
    )
    out_specs = (
        P("dp", "seq", None),
        P("dp", "seq", None),
        P("dp", "seq", None),
        P("dp", "seq", None),
        P(),
        P(),
    )
    return jax.shard_map(
        per_device, mesh=mesh, in_specs=in_specs, out_specs=out_specs, check_vma=False
    )
```

profile of v0, /device:TPU:0, one launch (start us, length us, event | category | flops | bytes accessed | tf_op | source)
XLA Modules:
  0.0 838.4 jit_solution(14274396235689733469)
XLA Ops:
  15.6 20.2 %slice.1381 = bf16[1,128,2048]{1,2,0:T(8,128)(2,1)S(1)} slice(bf16[1,256,2048]{1,2,0:T(8,128)(2,1)S(1)} %bitcast.1224), slice={[0:1:1], [0:256:2], [0:2048:1]} | slice | bytes 1048576 | tf_op jit(solution)/shard_map/slice | solution.py:25
  35.8 20.2 %slice.1383 = bf16[1,128,2048]{1,2,0:T(8,128)(2,1)S(1)} slice(bf16[1,256,2048]{1,2,0:T(8,128)(2,1)S(1)} %bitcast.1225), slice={[0:1:1], [1:256:2], [0:2048:1]} | slice | bytes 1048576 | tf_op jit(solution)/shard_map/slice | solution.py:25
  59.7 20.9 %slice.1377 = bf16[1,128,2048]{1,2,0:T(8,128)(2,1)S(1)} slice(bf16[1,258,2048]{1,2,0:T(8,128)(2,1)} %pad_maximum_fusion.8), slice={[0:1:1], [0:256:2], [0:2048:1]} | slice | bytes 1048576 | tf_op jit(solution)/shard_map/slice | solution.py:23
  80.5 21.4 %slice.1379 = bf16[1,128,2048]{1,2,0:T(8,128)(2,1)} slice(bf16[1,258,2048]{1,2,0:T(8,128)(2,1)} %pad_maximum_fusion.8), slice={[0:1:1], [1:257:2], [0:2048:1]} | slice | bytes 1048576 | tf_op jit(solution)/shard_map/slice | solution.py:25
  110.7 10.9 %slice.1390 = bf16[1,64,2048]{1,2,0:T(8,128)(2,1)S(1)} slice(bf16[1,128,2048]{1,2,0:T(8,128)(2,1)S(1)} %fusion.123), slice={[0:1:1], [0:128:2], [0:2048:1]} | slice | bytes 524288 | tf_op jit(solution)/shard_map/slice | solution.py:25
  121.6 11.0 %slice.1392 = bf16[1,64,2048]{1,2,0:T(8,128)(2,1)S(1)} slice(bf16[1,128,2048]{1,2,0:T(8,128)(2,1)S(1)} %fusion.123), slice={[0:1:1], [1:128:2], [0:2048:1]} | slice | bytes 524288 | tf_op jit(solution)/shard_map/slice | solution.py:25
  135.5 11.4 %slice.1386 = bf16[1,64,2048]{1,2,0:T(8,128)(2,1)S(1)} slice(bf16[1,130,2048]{1,2,0:T(8,128)(2,1)} %pad_maximum_fusion.11), slice={[0:1:1], [0:128:2], [0:2048:1]} | slice | bytes 524288 | tf_op jit(solution)/shard_map/slice | solution.py:23
  146.9 12.1 %slice.1388 = bf16[1,64,2048]{1,2,0:T(8,128)(2,1)} slice(bf16[1,130,2048]{1,2,0:T(8,128)(2,1)} %pad_maximum_fusion.11), slice={[0:1:1], [1:129:2], [0:2048:1]} | slice | bytes 524288 | tf_op jit(solution)/shard_map/slice | solution.py:25
  166.9 9.9 %collective-permute-done.4 = bf16[1,64,2048]{1,2,0:T(8,128)(2,1)} collective-permute-done((bf16[1,64,2048]{1,2,0:T(8,128)(2,1)}, bf16[1,64,2048]{1,2,0:T(8,128)(2,1)}, u32[]{:S(2)}, u32[]{:S(2)}) %collective-permute-start.4) | collective-permute-done | bytes 262176 | tf_op jit(solution)/shard_map/ppermute | solution.py:18
  186.8 5.5 collective-permute-start.18
  200.6 10.9 %slice.1399 = bf16[1,64,2048]{1,2,0:T(8,128)(2,1)S(1)} slice(bf16[1,128,2048]{1,2,0:T(8,128)(2,1)S(1)} %maximum_select_fusion), slice={[0:1:1], [0:128:2], [0:2048:1]} | slice | bytes 524288 | tf_op jit(solution)/shard_map/slice | solution.py:25
  211.5 11.0 %slice.1401 = bf16[1,64,2048]{1,2,0:T(8,128)(2,1)S(1)} slice(bf16[1,128,2048]{1,2,0:T(8,128)(2,1)S(1)} %maximum_select_fusion), slice={[0:1:1], [1:128:2], [0:2048:1]} | slice | bytes 524288 | tf_op jit(solution)/shard_map/slice | solution.py:25
  225.4 11.8 %slice.1395 = bf16[1,64,2048]{1,2,0:T(8,128)(2,1)} slice(bf16[1,130,2048]{1,2,0:T(8,128)(2,1)} %pad_maximum_fusion.12), slice={[0:1:1], [0:128:2], [0:2048:1]} | slice | bytes 524288 | tf_op jit(solution)/shard_map/slice | solution.py:23
  237.2 11.9 %slice.1397 = bf16[1,64,2048]{1,2,0:T(8,128)(2,1)} slice(bf16[1,130,2048]{1,2,0:T(8,128)(2,1)} %pad_maximum_fusion.12), slice={[0:1:1], [1:129:2], [0:2048:1]} | slice | bytes 524288 | tf_op jit(solution)/shard_map/slice | solution.py:25
  259.1 8.9 %collective-permute-done.7 = bf16[1,64,2048]{1,2,0:T(8,128)(2,1)S(1)} collective-permute-done((bf16[1,64,2048]{1,2,0:T(8,128)(2,1)S(1)}, bf16[1,64,2048]{1,2,0:T(8,128)(2,1)S(1)}, u32[]{:S(2)}, u32[]{:S(2)}) %collective-permute-start.7) | collective-permute-done | bytes 262176 | tf_op jit(solution)/shard_map/ppermute | solution.py:18
  304.3 264.9 %while.91 = (s32[]{:T(128)}, bf16[1,2,128,8,128]{4,3,2,1,0:T(8,128)(2,1)}, bf16[1,2,128,8,128]{4,3,2,1,0:T(8,128)(2,1)}, f32[1,4,128,8,2,128]{5,4,3,0,2,1:T(2,12...) while((s32[]{:T(128)}, ...), condition=%wide.region_12.13_spmd.clone.clone, body=%wide.region_0.12_spmd.clone.clone.sunk | while | flops 919731392 | bytes 101991640 | solution.py:269
  570.5 5.8 scatter-add.36
  577.7 6.3 collective-permute-start.11
  619.7 6.1 collective-permute-done.12
  634.3 6.1 scatter-add.39
  646.7 5.9 collective-permute-done.13
  658.5 6.0 collective-permute-done.15
  672.2 5.8 scatter-add.40
  713.0 111.6 %all-reduce.17.cloned.1.call-done = f32[3,4,8,2,128]{4,3,2,1,0:T(2,128)} async-done(((f32[3,4,8,2,128]{4,3,2,1,0:T(2,128)}), f32[3,4,8,2,128]{4,3,2,1,0:T(2,128)}) %all-reduce.17.cloned.1.call-update) | async-done | bytes 98320 | tf_op jit(solution)/shard_map/psum | solution.py:374
  (857 shorter events, 468.2 us)
Async XLA Ops:
  7.2 817.5 %all-reduce.17.cloned.1.call-start = ((), (), s32[]{:S(2)}) async-start(), calls=%async_computation | async-start | bytes 196608 | tf_op jit(solution)/shard_map/psum | solution.py:374
  10.7 46.2 %collective-permute-start = (bf16[1,128,2048]{1,2,0:T(8,128)(2,1)S(1)}, bf16[1,128,2048]{1,2,0:T(8,128)(2,1)S(1)}, u32[]{:S(2)}, u32[]{:S(2)}) collective-permute-start(bf16[1,128,2048]{1,2,0:T(8,128)(2,1)S(1)} %get-tuple-element.1401), channel_id=1, source_target_pairs={{0,4},{4,8},{8,12},{12,16},{16,20},{20,24},{24,28},{1,5},{5,9},{9,... | collective-permute-start | bytes 1572872 | tf_op jit(solution)/shard_map/ppermute | solution.py:14
  104.8 27.8 %collective-permute-start.2 = (bf16[1,128,2048]{1,2,0:T(8,128)(2,1)S(1)}, bf16[1,128,2048]{1,2,0:T(8,128)(2,1)}, u32[]{:S(2)}, u32[]{:S(2)}) collective-permute-start(bf16[1,128,2048]{1,2,0:T(8,128)(2,1)S(1)} %fusion.123), channel_id=1, source_target_pairs={{0,4},{4,8},{8,12},{12,16},{16,20},{20,24},{24,28},{1,5},{5,9},{9,... | collective-permute-start | bytes 1572872 | tf_op jit(solution)/shard_map/ppermute | solution.py:14
  109.1 146.1 %collective-permute-start.1 = (bf16[1,128,2048]{1,2,0:T(8,128)(2,1)}, bf16[1,128,2048]{1,2,0:T(8,128)(2,1)}, u32[]{:S(2)}, u32[]{:S(2)}) collective-permute-start(bf16[1,128,2048]{1,2,0:T(8,128)(2,1)} %get-tuple-element.1402), channel_id=1, source_target_pairs={{4,0},{8,4},{12,8},{16,12},{20,16},{24,20},{28,24},{5,1},{9,5},{13... | collective-permute-start | bytes 1572872 | tf_op jit(solution)/shard_map/ppermute | solution.py:14
  162.7 14.0 %collective-permute-start.4 = (bf16[1,64,2048]{1,2,0:T(8,128)(2,1)}, bf16[1,64,2048]{1,2,0:T(8,128)(2,1)}, u32[]{:S(2)}, u32[]{:S(2)}) collective-permute-start(bf16[1,64,2048]{1,2,0:T(8,128)(2,1)} %fusion.131), channel_id=1, source_target_pairs={{0,4},{4,0},{8,12},{12,8},{16,20},{20,16},{24,28},{28,24},{1,5},{5... | collective-permute-start | bytes 786440 | tf_op jit(solution)/shard_map/ppermute | solution.py:18
  178.9 43.6 %collective-permute-start.5 = (bf16[1,128,2048]{1,2,0:T(8,128)(2,1)S(1)}, bf16[1,128,2048]{1,2,0:T(8,128)(2,1)}, u32[]{:S(2)}, u32[]{:S(2)}) collective-permute-start(bf16[1,128,2048]{1,2,0:T(8,128)(2,1)S(1)} %maximum_select_fusion), channel_id=1, source_target_pairs={{0,8},{4,12},{8,16},{12,20},{16,24},{20,28},{1,9},{5,13},{9,17},{1... | collective-permute-start | bytes 1572872 | tf_op jit(solution)/shard_map/ppermute | solution.py:14
  184.3 90.1 %collective-permute-start.20 = (bf16[1,128,2048]{1,2,0:T(8,128)(2,1)}, bf16[1,128,2048]{1,2,0:T(8,128)(2,1)}, u32[]{:S(2)}, u32[]{:S(2)}) collective-permute-start(bf16[1,128,2048]{1,2,0:T(8,128)(2,1)} %pad_maximum_fusion.16), channel_id=1, source_target_pairs={{4,0},{8,4},{12,8},{16,12},{20,16},{24,20},{28,24},{5,1},{9,5},{13... | collective-permute-start | bytes 1572872 | tf_op jit(solution)/shard_map/ppermute | solution.py:14
  186.8 94.7 %collective-permute-start.18 = (bf16[1,128,2048]{1,2,0:T(8,128)(2,1)}, bf16[1,128,2048]{1,2,0:T(8,128)(2,1)}, u32[]{:S(2)}, u32[]{:S(2)}) collective-permute-start(bf16[1,128,2048]{1,2,0:T(8,128)(2,1)} %pad_maximum_fusion.15), channel_id=1, source_target_pairs={{0,4},{4,8},{8,12},{12,16},{16,20},{20,24},{24,28},{1,5},{5,9},{9,... | collective-permute-start | bytes 1572872 | tf_op jit(solution)/shard_map/ppermute | solution.py:14
  198.8 84.6 %collective-permute-start.3 = (bf16[1,128,2048]{1,2,0:T(8,128)(2,1)S(1)}, bf16[1,128,2048]{1,2,0:T(8,128)(2,1)}, u32[]{:S(2)}, u32[]{:S(2)}) collective-permute-start(bf16[1,128,2048]{1,2,0:T(8,128)(2,1)S(1)} %fusion.123), channel_id=1, source_target_pairs={{4,0},{8,4},{12,8},{16,12},{20,16},{24,20},{28,24},{5,1},{9,5},{13... | collective-permute-start | bytes 1572872 | tf_op jit(solution)/shard_map/ppermute | solution.py:14
  252.3 15.7 %collective-permute-start.7 = (bf16[1,64,2048]{1,2,0:T(8,128)(2,1)S(1)}, bf16[1,64,2048]{1,2,0:T(8,128)(2,1)S(1)}, u32[]{:S(2)}, u32[]{:S(2)}) collective-permute-start(bf16[1,64,2048]{1,2,0:T(8,128)(2,1)S(1)} %fusion.139), channel_id=1, source_target_pairs={{0,8},{4,12},{8,0},{12,4},{16,24},{20,28},{24,16},{28,20},{1,9},{5... | collective-permute-start | bytes 786440 | tf_op jit(solution)/shard_map/ppermute | solution.py:18
  257.8 34.5 %collective-permute-start.6 = (bf16[1,128,2048]{1,2,0:T(8,128)(2,1)S(1)}, bf16[1,128,2048]{1,2,0:T(8,128)(2,1)S(1)}, u32[]{:S(2)}, u32[]{:S(2)}) collective-permute-start(bf16[1,128,2048]{1,2,0:T(8,128)(2,1)S(1)} %maximum_select_fusion), channel_id=1, source_target_pairs={{8,0},{12,4},{16,8},{20,12},{24,16},{28,20},{9,1},{13,5},{17,9},{2... | collective-permute-start | bytes 1572872 | tf_op jit(solution)/shard_map/ppermute | solution.py:14
  269.4 22.9 %collective-permute-start.8 = (bf16[1,128,2048]{1,2,0:T(8,128)(2,1)}, bf16[1,128,2048]{1,2,0:T(8,128)(2,1)}, u32[]{:S(2)}, u32[]{:S(2)}) collective-permute-start(bf16[1,128,2048]{1,2,0:T(8,128)(2,1)} %maximum_select_fusion.1), channel_id=1, source_target_pairs={{0,16},{4,20},{8,24},{12,28},{1,17},{5,21},{9,25},{13,29},{2,18},{... | collective-permute-start | bytes 1572872 | tf_op jit(solution)/shard_map/ppermute | solution.py:14
  274.4 19.9 %collective-permute-start.9 = (bf16[1,128,2048]{1,2,0:T(8,128)(2,1)}, bf16[1,128,2048]{1,2,0:T(8,128)(2,1)}, u32[]{:S(2)}, u32[]{:S(2)}) collective-permute-start(bf16[1,128,2048]{1,2,0:T(8,128)(2,1)} %maximum_select_fusion.1), channel_id=1, source_target_pairs={{16,0},{20,4},{24,8},{28,12},{17,1},{21,5},{25,9},{29,13},{18,2},{... | collective-permute-start | bytes 1572872 | tf_op jit(solution)/shard_map/ppermute | solution.py:14
  576.4 37.8 %collective-permute-start.10 = (bf16[1,128,2048]{1,2,0:T(8,128)(2,1)}, bf16[1,128,2048]{1,2,0:T(8,128)(2,1)S(1)}, u32[]{:S(2)}, u32[]{:S(2)}) collective-permute-start(bf16[1,128,2048]{1,2,0:T(8,128)(2,1)} %scatter-add.36), channel_id=1, source_target_pairs={{16,0},{20,4},{24,8},{28,12},{17,1},{21,5},{25,9},{29,13},{18,2},{... | collective-permute-start | bytes 1572872 | tf_op jit(solution)/shard_map/ppermute | solution.py:14
  577.7 36.5 %collective-permute-start.11 = (bf16[1,128,2048]{1,2,0:T(8,128)(2,1)S(1)}, bf16[1,128,2048]{1,2,0:T(8,128)(2,1)}, u32[]{:S(2)}, u32[]{:S(2)}) collective-permute-start(bf16[1,128,2048]{1,2,0:T(8,128)(2,1)S(1)} %bitcast.1263), channel_id=1, source_target_pairs={{0,16},{4,20},{8,24},{12,28},{1,17},{5,21},{9,25},{13,29},{2,18},{... | collective-permute-start | bytes 1572872 | tf_op jit(solution)/shard_map/ppermute | solution.py:14
  584.0 62.7 %collective-permute-start.14 = (bf16[1,128,2048]{1,2,0:T(8,128)(2,1)}, bf16[1,128,2048]{1,2,0:T(8,128)(2,1)}, u32[]{:S(2)}, u32[]{:S(2)}) collective-permute-start(bf16[1,128,2048]{1,2,0:T(8,128)(2,1)} %bitcast.29), channel_id=1, source_target_pairs={{0,8},{4,12},{8,16},{12,20},{16,24},{20,28},{1,9},{5,13},{9,17},{1... | collective-permute-start | bytes 1572872 | tf_op jit(solution)/shard_map/ppermute | solution.py:14
  590.8 95.9 %collective-permute-start.16 = (bf16[1,128,2048]{1,2,0:T(8,128)(2,1)}, bf16[1,128,2048]{1,2,0:T(8,128)(2,1)}, u32[]{:S(2)}, u32[]{:S(2)}) collective-permute-start(bf16[1,128,2048]{1,2,0:T(8,128)(2,1)} %copy.975), channel_id=1, source_target_pairs={{0,4},{4,8},{8,12},{12,16},{16,20},{20,24},{24,28},{1,5},{5,9},{9,... | collective-permute-start | bytes 1572872 | tf_op jit(solution)/shard_map/ppermute | solution.py:14
  594.1 15.1 %collective-permute-start.21 = (bf16[1,2,8,128]{3,2,1,0:T(8,128)(2,1)S(1)}, bf16[1,2,8,128]{3,2,1,0:T(8,128)(2,1)S(1)}, u32[]{:S(2)}, u32[]{:S(2)}) collective-permute-start(bf16[1,2,8,128]{3,2,1,0:T(8,128)(2,1)S(1)} %pad_maximum_fusion.20), channel_id=1, source_target_pairs={{4,0},{8,4},{12,8},{16,12},{20,16},{24,20},{28,24},{5,1},{9,5},{13... | collective-permute-start | bytes 12296 | tf_op jit(solution)/shard_map/ppermute | solution.py:14
  609.2 34.9 %collective-permute-start.19 = (bf16[1,2,8,128]{3,2,1,0:T(8,128)(2,1)S(1)}, bf16[1,2,8,128]{3,2,1,0:T(8,128)(2,1)S(1)}, u32[]{:S(2)}, u32[]{:S(2)}) collective-permute-start(bf16[1,2,8,128]{3,2,1,0:T(8,128)(2,1)S(1)} %pad_maximum_fusion.19), channel_id=1, source_target_pairs={{0,4},{4,8},{8,12},{12,16},{16,20},{20,24},{24,28},{1,5},{5,9},{9,... | collective-permute-start | bytes 12296 | tf_op jit(solution)/shard_map/ppermute | solution.py:14
  616.4 9.5 %collective-permute-start.12 = (bf16[1,64,2048]{1,2,0:T(8,128)(2,1)}, bf16[1,64,2048]{1,2,0:T(8,128)(2,1)}, u32[]{:S(2)}, u32[]{:S(2)}) collective-permute-start(bf16[1,64,2048]{1,2,0:T(8,128)(2,1)} %select_convert_fusion.1), channel_id=1, source_target_pairs={{0,8},{4,12},{8,0},{12,4},{16,24},{20,28},{24,16},{28,20},{1,9},{5... | collective-permute-start | bytes 786440 | tf_op jit(solution)/shard_map/ppermute | solution.py:18
  641.2 11.4 %collective-permute-start.13 = (bf16[1,128,2048]{1,2,0:T(8,128)(2,1)}, bf16[1,128,2048]{1,2,0:T(8,128)(2,1)}, u32[]{:S(2)}, u32[]{:S(2)}) collective-permute-start(bf16[1,128,2048]{1,2,0:T(8,128)(2,1)} %convert_element_type.291), channel_id=1, source_target_pairs={{8,0},{12,4},{16,8},{20,12},{24,16},{28,20},{9,1},{13,5},{17,9},{2... | collective-permute-start | bytes 1572872 | tf_op jit(solution)/shard_map/ppermute | solution.py:14
  655.0 9.5 %collective-permute-start.15 = (bf16[1,64,2048]{1,2,0:T(8,128)(2,1)}, bf16[1,64,2048]{1,2,0:T(8,128)(2,1)}, u32[]{:S(2)}, u32[]{:S(2)}) collective-permute-start(bf16[1,64,2048]{1,2,0:T(8,128)(2,1)} %select_convert_fusion), channel_id=1, source_target_pairs={{0,4},{4,0},{8,12},{12,8},{16,20},{20,16},{24,28},{28,24},{1,5},{5... | collective-permute-start | bytes 786440 | tf_op jit(solution)/shard_map/ppermute | solution.py:18
  678.0 11.4 %collective-permute-start.17 = (bf16[1,128,2048]{1,2,0:T(8,128)(2,1)}, bf16[1,128,2048]{1,2,0:T(8,128)(2,1)}, u32[]{:S(2)}, u32[]{:S(2)}) collective-permute-start(bf16[1,128,2048]{1,2,0:T(8,128)(2,1)} %scatter-add.40), channel_id=1, source_target_pairs={{4,0},{8,4},{12,8},{16,12},{20,16},{24,20},{28,24},{5,1},{9,5},{13... | collective-permute-start | bytes 1572872 | tf_op jit(solution)/shard_map/ppermute | solution.py:14
  706.9 120.2 %collective-permute-start.22 = (bf16[1,128,2048]{2,1,0:T(8,128)(2,1)}, bf16[1,128,2048]{2,1,0:T(8,128)(2,1)}, u32[]{:S(2)}, u32[]{:S(2)}) collective-permute-start(bf16[1,128,2048]{2,1,0:T(8,128)(2,1)} %scatter-add.44.clone), channel_id=1, source_target_pairs={{4,0},{8,4},{12,8},{16,12},{20,16},{24,20},{28,24},{5,1},{9,5},{13... | collective-permute-start | bytes 1572872 | tf_op jit(solution)/shard_map/ppermute | solution.py:14
  (160 other events, 2005.3 us)
Sparse Core Ops, SparseCore 0:
  706.2 118.4 all-reduce.16
where the time goes:
time: 854 us; the launch traced here: 838 us
  local copies, waits for them, and re-layouts  333 us (39%)
  matrix products  165 us (19%)
  waiting for transfers between devices  153 us (18%)
  other arithmetic  109 us (13%)
  starting transfers between devices  60.1 us (7%)
  between operations  15.5 us (2%)
    slice x9, local copies, waits for them, and re-layouts, coarsen(): extended[:, offset:offset + 2 * out_rows:2].astype(jnp.float32)  130 us
    psum x1, waiting for transfers between devices, per_device(): lax.psum(jnp.stack(weight_grads), ('seq', 'dp'))  112 us
    ppermute x19, starting transfers between devices, passed_along(): lax.ppermute(value, axis, [(source, source + steps) for source in range(i...  54.4 us
    dot_general x36, matrix products, head_group(): jnp.einsum('bnrqhe,bnkhe->bnrhqk', do_view, key_blocks[..., 1, :], prefer...  53.2 us
    slice x3, local copies, waits for them, and re-layouts, coarsen(): summed = weight[0] * extended[:, 0:2 * out_rows:2].astype(jnp.float32)  44 us
    ppermute x4, waiting for transfers between devices, partner_2(): lax.ppermute(array, axis, [(i, i ^ 1 << distance) for i in range(lax.axis...  31 us
    dot_general x36, matrix products, head_group(): jnp.einsum('bnrqhe,bnkhe->bnrhqk', q_view, key_blocks[..., 0, :], preferr...  31 us
    dot_general x36, matrix products, head_group(): jnp.einsum('bnrhqk,bnkhe->bnrqhe', p_slice, key_blocks[..., 1, :], prefer...  28.3 us
  transfers between devices with their start and end apart: 24, of which 8 were waited for; matrix products, arithmetic and copies ran while one was open for 30% of the time, Pallas kernels for 0%

commit v1 on v0

--- a/solution.py
+++ b/solution.py
@@ -1,6 +1,10 @@
+import functools
+
 import jax
 import jax.numpy as jnp
 from jax import lax
+from jax.experimental import pallas as pl
+from jax.experimental.pallas import tpu as pltpu
 from jax.sharding import PartitionSpec as P
 
 HEADS = 8
@@ -379,6 +383,251 @@
     return (attended, grad_query, grad_key, grad_value, grad_conv_key, grad_conv_value)
 
 
+LOG2E = 1.4426950408889634
+MASKED = -1e30
+
+
+def level_bases(blocks, levels):
+    bases, offset = [], 0
+    for level_id in range(levels + 1):
+        bases.append(offset)
+        offset += (blocks >> level_id) + 2
+    return bases, offset
+
+
+def build_levels(load_pair, weight, bases, blocks, levels, wide_ref, low_ref, turned_ref):
+    zero_wide = jnp.zeros((BLOCK, HEAD_DIM), jnp.float32)
+    zero_low = jnp.zeros((BLOCK, HEAD_DIM), jnp.bfloat16)
+    for level_id in range(levels + 1):
+        for pad in (bases[level_id], bases[level_id] + (blocks >> level_id) + 1):
+            wide_ref[pad * BLOCK : (pad + 1) * BLOCK] = zero_wide
+            low_ref[pad] = zero_low
+            turned_ref[pad] = zero_low
+
+    def put(index, low):
+        wide = low.astype(jnp.float32)
+        wide_ref[pl.ds(pl.multiple_of(index * BLOCK, BLOCK), BLOCK)] = wide
+        low_ref[index] = low
+        turned_ref[index] = wide.T.astype(jnp.bfloat16)
+
+    def put_pair(pair, carry):
+        rows = load_pair(pair)
+        put(1 + 2 * pair, rows[:BLOCK])
+        put(2 + 2 * pair, rows[BLOCK:])
+        return carry
+
+    lax.fori_loop(0, blocks // 2, put_pair, 0)
+    for level_id in range(1, levels + 1):
+        for block in range(blocks >> level_id):
+            start = (bases[level_id - 1] + 1 + 2 * block) * BLOCK - 2
+            summed = jnp.zeros((BLOCK, HEAD_DIM), jnp.float32)
+            for tap in range(4):
+                row = 4 * (level_id - 1) + tap
+                summed = summed + weight(row) * wide_ref[pl.ds(start + tap, BLOCK, stride=2)]
+            put(bases[level_id] + 1 + block, summed.astype(jnp.bfloat16))
+
+
+def attend_pair(pair, q_rows, do_rows, bases, blocks, levels, keys, values, scratch):
+    key_low, key_turned, key_grad = keys
+    value_low, value_turned, value_grad = values
+    score_ref, dprob_ref = scratch
+    scale = HEAD_DIM**-0.5
+    two = 2 * BLOCK
+    q_turned = q_rows.astype(jnp.float32).T.astype(jnp.bfloat16)
+    do_turned = do_rows.astype(jnp.float32).T.astype(jnp.bfloat16)
+    lane = lax.broadcasted_iota(jnp.int32, (1, two), 1)
+    pairs = blocks // 2
+    places = [2 * pair, 2 * pair + 1, 2 * pair + 2, 2 * pair + 3]
+    spans = [
+        (0, jnp.where(pair > 0, BLOCK, 0)),
+        None,
+        None,
+        (jnp.where(pair + 1 < pairs, BLOCK, two), two),
+    ]
+    for level_id in range(1, levels + 1):
+        coarse_id = pair // 2 ** (level_id - 1)
+        places += [bases[level_id] + coarse_id, bases[level_id] + coarse_id + 2]
+        spans += [
+            (0, jnp.where(coarse_id >= 1, two, 0)),
+            (0, jnp.where(coarse_id + 1 < blocks >> level_id, two, 0)),
+        ]
+    row_max = jnp.full((1, two), MASKED, jnp.float32)
+    for piece, place in enumerate(places):
+        score = jnp.dot(key_low[place], q_turned, preferred_element_type=jnp.float32)
+        if spans[piece] is not None:
+            first, last = spans[piece]
+            score = jnp.where((lane >= first) & (lane < last), score, MASKED)
+        score_ref[piece] = score
+        row_max = jnp.maximum(row_max, jnp.max(score, 0, keepdims=True))
+    total = jnp.zeros((1, two), jnp.float32)
+    weighted = jnp.zeros((1, two), jnp.float32)
+    for piece, place in enumerate(places):
+        raised = jnp.exp2((score_ref[piece] - row_max) * (scale * LOG2E))
+        dprob = jnp.dot(value_low[place], do_turned, preferred_element_type=jnp.float32)
+        score_ref[piece] = raised
+        dprob_ref[piece] = dprob
+        total = total + jnp.sum(raised, 0, keepdims=True)
+        weighted = weighted + jnp.sum(raised * dprob, 0, keepdims=True)
+    inverse = 1.0 / total
+    delta = weighted * inverse
+    attended = jnp.zeros((HEAD_DIM, two), jnp.float32)
+    grad_q = jnp.zeros((HEAD_DIM, two), jnp.float32)
+    for piece in range(0, len(places), 2):
+        lows, dlows = [], []
+        for step in (piece, piece + 1):
+            rows = pl.ds(pl.multiple_of(places[step] * BLOCK, BLOCK), BLOCK)
+            probs = score_ref[step] * inverse
+            probs_low = probs.astype(jnp.bfloat16)
+            dscore = (probs * (dprob_ref[step] - delta)).astype(jnp.bfloat16)
+            value_grad[rows] += jnp.dot(probs_low, do_rows, preferred_element_type=jnp.float32)
+            key_grad[rows] += jnp.dot(dscore, q_rows, preferred_element_type=jnp.float32)
+            lows.append(probs_low)
+            dlows.append(dscore)
+        here, there = places[piece], places[piece + 1]
+        value_two = jnp.concatenate([value_turned[here], value_turned[there]], 1)
+        key_two = jnp.concatenate([key_turned[here], key_turned[there]], 1)
+        attended = attended + jnp.dot(
+            value_two, jnp.concatenate(lows, 0), preferred_element_type=jnp.float32
+        )
+        grad_q = grad_q + jnp.dot(
+            key_two, jnp.concatenate(dlows, 0), preferred_element_type=jnp.float32
+        )
+    return attended.T.astype(jnp.bfloat16), (grad_q * scale).T.astype(jnp.bfloat16)
+
+
+def coarsen_gradients(weight, bases, blocks, levels, wide_ref, grad_ref, put_weight_grad):
+    for level_id in range(levels, 0, -1):
+        tap_sums = [jnp.zeros((1, HEAD_DIM), jnp.float32) for _ in range(4)]
+        for block in range(blocks >> level_id):
+            start = (bases[level_id] + 1 + block) * BLOCK
+            upstream = grad_ref[start : start + BLOCK]
+            following = grad_ref[start + 1 : start + 1 + BLOCK]
+            below = (bases[level_id - 1] + 1 + 2 * block) * BLOCK
+            taps = [weight(4 * (level_id - 1) + tap) for tap in range(4)]
+            grad_ref[pl.ds(below, BLOCK, stride=2)] += taps[2] * upstream + taps[0] * following
+            grad_ref[pl.ds(below + 1, BLOCK, stride=2)] += taps[3] * upstream + taps[1] * following
+            for tap in range(4):
+                tap_sums[tap] = tap_sums[tap] + jnp.sum(
+                    upstream * wide_ref[pl.ds(below - 2 + tap, BLOCK, stride=2)], 0, keepdims=True
+                )
+        for tap in range(4):
+            put_weight_grad(4 * (level_id - 1) + tap, tap_sums[tap])
+
+
+def head_kernel(
+    levels,
+    rows_ref,
+    conv_ref,
+    out_ref,
+    conv_grad_ref,
+    key_wide,
+    key_low,
+    key_turned,
+    key_grad,
+    value_wide,
+    value_low,
+    value_turned,
+    value_grad,
+    score_ref,
+    dprob_ref,
+):
+    pairs = rows_ref.shape[0]
+    blocks = 2 * pairs
+    bases, _ = level_bases(blocks, levels)
+    taps = 4 * levels
+    scale = HEAD_DIM**-0.5
+
+    def key_weight(row):
+        return conv_ref[row : row + 1]
+
+    def value_weight(row):
+        return conv_ref[taps + row : taps + row + 1]
+
+    shape = (bases, blocks, levels)
+    build_levels(lambda pair: rows_ref[pair, 1], key_weight, *shape, key_wide, key_low, key_turned)
+    build_levels(
+        lambda pair: rows_ref[pair, 2], value_weight, *shape, value_wide, value_low, value_turned
+    )
+    key_grad[...] = jnp.zeros_like(key_grad)
+    value_grad[...] = jnp.zeros_like(value_grad)
+
+    def step(pair, carry):
+        attended, grad_q = attend_pair(
+            pair,
+            rows_ref[pair, 0],
+            rows_ref[pair, 3],
+            *shape,
+            (key_low, key_turned, key_grad),
+            (value_low, value_turned, value_grad),
+            (score_ref, dprob_ref),
+        )
+        out_ref[pair, 0] = attended
+        out_ref[pair, 1] = grad_q
+        return carry
+
+    lax.fori_loop(0, pairs, step, 0)
+
+    def put_key(row, value):
+        conv_grad_ref[row : row + 1] = value * scale
+
+    def put_value(row, value):
+        conv_grad_ref[taps + row : taps + row + 1] = value
+
+    coarsen_gradients(key_weight, *shape, key_wide, key_grad, put_key)
+    coarsen_gradients(value_weight, *shape, value_wide, value_grad, put_value)
+
+    def finish(pair, carry):
+        rows = pl.ds(pl.multiple_of((1 + 2 * pair) * BLOCK, BLOCK), 2 * BLOCK)
+        out_ref[pair, 2] = (key_grad[rows] * scale).astype(jnp.bfloat16)
+        out_ref[pair, 3] = value_grad[rows].astype(jnp.bfloat16)
+        return carry
+
+    lax.fori_loop(0, pairs, finish, 0)
+
+
+def stack_scratch(blocks, levels):
+    total = level_bases(blocks, levels)[1]
+    flat = pltpu.VMEM((total * BLOCK, HEAD_DIM), jnp.float32)
+    low = pltpu.VMEM((total, BLOCK, HEAD_DIM), jnp.bfloat16)
+    return [flat, low, low, flat]
+
+
+def one_head(rows, conv, levels):
+    pairs = rows.shape[0]
+    pieces = 4 + 2 * levels
+    scores = pltpu.VMEM((pieces, BLOCK, 2 * BLOCK), jnp.float32)
+    return pl.pallas_call(
+        functools.partial(head_kernel, levels),
+        out_shape=(
+            jax.ShapeDtypeStruct(rows.shape, jnp.bfloat16),
+            jax.ShapeDtypeStruct(conv.shape, jnp.float32),
+        ),
+        in_specs=[pl.BlockSpec(memory_space=pltpu.VMEM)] * 2,
+        out_specs=[pl.BlockSpec(memory_space=pltpu.VMEM)] * 2,
+        scratch_shapes=stack_scratch(2 * pairs, levels) * 2 + [scores, scores],
+        compiler_params=pltpu.CompilerParams(vmem_limit_bytes=48 * 2**20),
+    )(rows, conv)
+
+
+def per_device_heads(queries, key_rows, value_rows, conv_key, conv_value, grad_out):
+    tok_rows = queries.shape[1]
+    levels = conv_key.shape[0]
+    head = lax.axis_index("seq")
+    stacked = jnp.stack([queries[0], key_rows[0], value_rows[0], grad_out[0]])
+    split = stacked.reshape(4, tok_rows, HEADS, HEAD_DIM).transpose(2, 0, 1, 3)
+    rows = lax.all_to_all(split, "seq", 0, 0)
+    conv = jnp.concatenate([conv_key, conv_value], 0).reshape(8 * levels, HEADS * HEAD_DIM)
+    conv_here = lax.dynamic_slice_in_dim(conv, head * HEAD_DIM, HEAD_DIM, 1)
+    outs, conv_grad = one_head(rows, conv_here, levels)
+    back = lax.all_to_all(outs, "seq", 0, 0)
+    whole = back.transpose(1, 2, 0, 3).reshape(4, 1, tok_rows, HEADS * HEAD_DIM)
+    placed = lax.dynamic_update_slice_in_dim(
+        jnp.zeros_like(conv), conv_grad, head * HEAD_DIM, 1
+    )
+    conv_sum = lax.psum(placed, ("seq", "dp")).reshape(2, levels, 4, HEADS * HEAD_DIM)
+    return (whole[0], whole[1], whole[2], whole[3], conv_sum[0], conv_sum[1])
+
+
 def solution(mesh):
     in_specs = (
         P("dp", "seq", None),
@@ -396,6 +645,11 @@
         P(),
         P(),
     )
+    def chosen(*args):
+        seq_devices = lax.axis_size("seq")
+        fits = seq_devices == HEADS and args[0].shape[:2] == (1, 2 * BLOCK)
+        return (per_device_heads if fits else per_device)(*args)
+
     return jax.shard_map(
-        per_device, mesh=mesh, in_specs=in_specs, out_specs=out_specs, check_vma=False
-    )
+        chosen, mesh=mesh, in_specs=in_specs, out_specs=out_specs, check_vma=False
+    )

time: 854 us -> 257 us (0.30); the launches traced: 838 us -> 257 us
  local copies, waits for them, and re-layouts: 333 us -> 18.3 us
  matrix products: 165 us -> 0 us
  other arithmetic: 109 us -> 1.49 us
  starting transfers between devices: 60.1 us -> 11.1 us
  waiting for transfers between devices: 153 us -> 194 us
  Pallas kernels: 0 us -> 17.8 us
    slice x36 -> x6, local copies, waits for them, and re-layouts: 206 us -> 4.01 us  [per_device_heads(): return (whole[0], whole[1], whole[2], whole[3], conv_sum[0], conv_sum[1])]
    dot_general x222 -> x0, matrix products: 165 us -> none  [the longest x36 53.2 us: head_group(): jnp.einsum('bnrqhe,bnkhe->bnrhqk', do_view, key_blocks[..., 1, :], prefer...]
    ppermute x23 -> x0, starting transfers between devices: 60 us -> none  [the longest x19 54.4 us: passed_along(): lax.ppermute(value, axis, [(source, source + steps) for source in range(i...]
    all_to_all x0 -> x2, waiting for transfers between devices: none -> 48.1 us  [the longest x1 48.1 us: per_device_heads(): rows = lax.all_to_all(split, 'seq', 0, 0)]
    ppermute x23 -> x0, waiting for transfers between devices: 41.6 us -> none  [the longest x4 31 us: partner_2(): lax.ppermute(array, axis, [(i, i ^ 1 << distance) for i in range(lax.axis...]
    psum x1, waiting for transfers between devices: 112 us -> 146 us  [per_device_heads(): lax.psum(placed, ('seq', 'dp')).reshape(2, levels, 4, HEADS * HEAD_DIM)]
    dynamic_update_slice x28 -> x1, local copies, waits for them, and re-layouts: 28.5 us -> 0.01 us  [per_device_heads(): lax.dynamic_update_slice_in_dim(jnp.zeros_like(conv), conv_grad, head * H...]
    scatter-add x14 -> x0, other arithmetic: 20.1 us -> none  [the longest x12 18.4 us: head_group(): group_grads[source_id].at[:, offset:offset + block_count].add(pair_grad)]
  transfers between devices with their start and end apart: 24 -> 3, of which waited for: 8 -> 2; matrix products, arithmetic and copies ran while one was open for 30% -> 1% of each run, Pallas kernels for 0% -> 0%
where the time goes in v1:
time: 257 us
  waiting for transfers between devices  194 us (75%)
  local copies, waits for them, and re-layouts  18.3 us (7%)
  Pallas kernels  17.8 us (7%)
  between operations  14.2 us (6%)
  starting transfers between devices  11.1 us (4%)
    psum x1, waiting for transfers between devices, per_device_heads(): lax.psum(placed, ('seq', 'dp')).reshape(2, levels, 4, HEADS * HEAD_DIM)  146 us
    all_to_all x1, waiting for transfers between devices, per_device_heads(): rows = lax.all_to_all(split, 'seq', 0, 0)  48.1 us
    pallas_call x1, Pallas kernels, one_head(): pl.pallas_call(functools.partial(head_kernel, levels), out_shape=(jax.Sha...  17.8 us
    unnamed x22, local copies, waits for them, and re-layouts  10.6 us
    all_to_all x1, starting transfers between devices, per_device_heads(): rows = lax.all_to_all(split, 'seq', 0, 0)  7.38 us
  transfers between devices with their start and end apart: 3, of which 2 were waited for; matrix products, arithmetic and copies ran while one was open for 1% of the time, Pallas kernels for 0%

profile of v1, /device:TPU:0, one launch (start us, length us, event | category | flops | bytes accessed | tf_op | source)
XLA Modules:
  0.0 256.5 jit_solution(16563887067104768162)
XLA Ops:
  7.2 1.3 copy.15
  8.5 1.2 copy.14
  9.8 1.0 copy.13
  10.8 1.0 copy.12
  11.8 1.5 pad_maximum_fusion
  13.2 2.4 copy.16
  15.7 7.4 %all-to-all-start = ((bf16[8,4,256,128]{3,2,1,0:T(8,128)(2,1)}), bf16[8,4,256,128]{3,2,1,0:T(8,128)(2,1)S(1)}, u32[]{:S(2)}, u32[]{:S(2)}) async-start(bf16[8,4,256,128]{3,2,1,0:T(8,128)(2,1)} %bitcast.8), calls=%async_computation | async-start | bytes 4194304 | tf_op jit(solution)/shard_map/all_to_all | solution.py:618
  23.2 48.1 %all-to-all-done.rows_ref = bf16[8,4,256,128]{3,2,1,0:T(8,128)(2,1)S(1)} async-done(((bf16[8,4,256,128]{3,2,1,0:T(8,128)(2,1)}), bf16[8,4,256,128]{3,2,1,0:T(8,128)(2,1)S(1)}, u32[]{:S(2)}, u32[]{:S(2)}) %all-to-all-start) | async-done | bytes 2097184 | tf_op jit(solution)/shard_map/all_to_all | solution.py:618
  71.3 17.8 %shard_map.109 = (bf16[8,4,256,128]{3,2,1,0:T(8,128)(2,1)S(1)}, f32[24,128]{1,0:T(8,128)S(1)}) custom-call(bf16[8,4,256,128]{3,2,1,0:T(8,128)(2,1)S(1)} %all-to-all-done.rows_ref, f32[24,128]{1,0:T(8,128)S(1)} %constant_dynamic-slice_fusion.conv_ref), custom_call_target="tpu_custom_call" | custom-call | tf_op jit(solution)/shard_map/pallas_call | solution.py:599
  89.1 1.3 copy-done
  90.4 3.6 %all-to-all-start.1 = ((bf16[8,4,256,128]{3,2,1,0:T(8,128)(2,1)}), bf16[8,4,256,128]{3,2,1,0:T(8,128)(2,1)S(1)}, u32[]{:S(2)}, u32[]{:S(2)}) async-start(bf16[8,4,256,128]{3,2,1,0:T(8,128)(2,1)} %copy-done), calls=%async_computation.1 | async-start | bytes 4194304 | tf_op jit(solution)/shard_map/all_to_all | solution.py:622
  94.2 0.6 copy-done.4
  94.8 145.5 %all-reduce.2.cloned.1.call-done = f32[24,1024]{1,0:T(8,128)} async-done(((f32[24,1024]{1,0:T(8,128)}), f32[24,1024]{1,0:T(8,128)}) %all-reduce.2.cloned.1.call-update) | async-done | bytes 98320 | tf_op jit(solution)/shard_map/psum | solution.py:627
  240.4 0.9 fusion.1
  241.3 0.6 squeeze.22
  241.9 0.6 squeeze.23
  242.6 1.2 fusion
  243.7 1.3 copy.17
  245.0 1.0 copy.21
  246.0 0.2 copy.18
  246.2 1.0 copy.22
  247.5 1.0 copy.23
  248.5 0.2 copy.20
  248.7 1.0 copy.24
  (21 shorter events, 0.4 us)
Async XLA Ops:
  7.2 2.6 %copy-start.2 = (bf16[1,256,1024]{2,1,0:T(8,128)(2,1)S(1)}, bf16[1,256,1024]{2,1,0:T(8,128)(2,1)}, u32[]{:S(2)}) copy-start(bf16[1,256,1024]{2,1,0:T(8,128)(2,1)} %param.7) | copy-start | bytes 1572868
  7.2 3.6 %copy-start.3 = (bf16[1,256,1024]{2,1,0:T(8,128)(2,1)S(1)}, bf16[1,256,1024]{2,1,0:T(8,128)(2,1)}, u32[]{:S(2)}) copy-start(bf16[1,256,1024]{2,1,0:T(8,128)(2,1)} %param.6) | copy-start | bytes 1572868
  15.7 7.4 %copy-start.5 = (f32[3,4,1024]{2,1,0:T(4,128)S(1)}, f32[3,4,1024]{2,1,0:T(4,128)}, u32[]{:S(2)}) copy-start(f32[3,4,1024]{2,1,0:T(4,128)} %param.10) | copy-start | bytes 147460
  15.7 7.4 %copy-start.6 = (f32[3,4,1024]{2,1,0:T(4,128)S(1)}, f32[3,4,1024]{2,1,0:T(4,128)}, u32[]{:S(2)}) copy-start(f32[3,4,1024]{2,1,0:T(4,128)} %param.9) | copy-start | bytes 147460
  15.7 55.6 %all-to-all-start = ((bf16[8,4,256,128]{3,2,1,0:T(8,128)(2,1)}), bf16[8,4,256,128]{3,2,1,0:T(8,128)(2,1)S(1)}, u32[]{:S(2)}, u32[]{:S(2)}) async-start(bf16[8,4,256,128]{3,2,1,0:T(8,128)(2,1)} %bitcast.8), calls=%async_computation | async-start | bytes 4194304 | tf_op jit(solution)/shard_map/all_to_all | solution.py:618
  89.1 1.3 copy-start
  90.4 152.1 %all-to-all-start.1 = ((bf16[8,4,256,128]{3,2,1,0:T(8,128)(2,1)}), bf16[8,4,256,128]{3,2,1,0:T(8,128)(2,1)S(1)}, u32[]{:S(2)}, u32[]{:S(2)}) async-start(bf16[8,4,256,128]{3,2,1,0:T(8,128)(2,1)} %copy-done), calls=%async_computation.1 | async-start | bytes 4194304 | tf_op jit(solution)/shard_map/all_to_all | solution.py:622
  94.1 146.3 %all-reduce.2.cloned.1.call-start = ((), (), s32[]{:S(2)}) async-start(), calls=%async_computation.2 | async-start | bytes 196608 | tf_op jit(solution)/shard_map/psum | solution.py:627
  94.1 0.6 copy-start.4
  243.7 2.3 copy-start.1
Sparse Core Ops, SparseCore 0:
  101.1 139.2 all-reduce.1

commit v2 on v1

--- a/solution.py
+++ b/solution.py
@@ -395,7 +395,7 @@
     return bases, offset
 
 
-def build_levels(load_pair, weight, bases, blocks, levels, wide_ref, low_ref, turned_ref):
+def build_levels(take_rows, weight, bases, blocks, levels, wide_ref, low_ref, turned_ref):
     zero_wide = jnp.zeros((BLOCK, HEAD_DIM), jnp.float32)
     zero_low = jnp.zeros((BLOCK, HEAD_DIM), jnp.bfloat16)
     for level_id in range(levels + 1):
@@ -410,8 +410,8 @@
         low_ref[index] = low
         turned_ref[index] = wide.T.astype(jnp.bfloat16)
 
-    def put_pair(pair, carry):
-        rows = load_pair(pair)
+    def put_pair(distance, carry):
+        pair, rows = take_rows(distance)
         put(1 + 2 * pair, rows[:BLOCK])
         put(2 + 2 * pair, rows[BLOCK:])
         return carry
@@ -514,12 +514,29 @@
             put_weight_grad(4 * (level_id - 1) + tap, tap_sums[tap])
 
 
+def columns(head):
+    return pl.ds(pl.multiple_of(head * HEAD_DIM, HEAD_DIM), HEAD_DIM)
+
+
 def head_kernel(
     levels,
+    ring,
+    groups,
+    q_hbm,
+    key_hbm,
+    value_hbm,
+    do_hbm,
+    conv_ref,
+    att_hbm,
+    grad_q_hbm,
+    grad_key_hbm,
+    grad_value_hbm,
+    conv_grad_ref,
     rows_ref,
-    conv_ref,
     out_ref,
-    conv_grad_ref,
+    conv_here,
+    conv_parts,
+    conv_total,
     key_wide,
     key_low,
     key_turned,
@@ -530,28 +547,131 @@
     value_grad,
     score_ref,
     dprob_ref,
+    in_send,
+    in_recv,
+    out_send,
+    out_recv,
+    part_send,
+    part_recv,
+    total_send,
+    total_recv,
 ):
-    pairs = rows_ref.shape[0]
-    blocks = 2 * pairs
+    me = lax.axis_index("seq")
+    group = lax.axis_index("dp")
+    blocks = 2 * ring
     bases, _ = level_bases(blocks, levels)
     taps = 4 * levels
     scale = HEAD_DIM**-0.5
+    sources = (q_hbm, key_hbm, value_hbm, do_hbm)
+    results = (att_hbm, grad_q_hbm, grad_key_hbm, grad_value_hbm)
+
+    def after(distance):
+        return lax.rem(me + distance, ring)
+
+    def before(distance):
+        return lax.rem(me + ring - distance, ring)
+
+    barrier = pltpu.get_barrier_semaphore()
+    for distance in range(1, ring):
+        pl.semaphore_signal(
+            barrier,
+            inc=1,
+            device_id={"seq": after(distance)},
+            device_id_type=pl.DeviceIdType.MESH,
+        )
+    for distance in range(1, groups):
+        pl.semaphore_signal(
+            barrier,
+            inc=1,
+            device_id={"dp": lax.rem(group + distance, groups)},
+            device_id_type=pl.DeviceIdType.MESH,
+        )
+    pl.semaphore_wait(barrier, ring + groups - 2)
+
+    def inbound(array, distance, landing):
+        return pltpu.make_async_remote_copy(
+            src_ref=sources[array].at[0, :, columns(after(distance))],
+            dst_ref=rows_ref.at[landing, array],
+            send_sem=in_send.at[array, distance],
+            recv_sem=in_recv.at[array, distance],
+            device_id={"seq": after(distance)},
+            device_id_type=pl.DeviceIdType.MESH,
+        )
+
+    def inbound_own(array):
+        return pltpu.make_async_copy(
+            sources[array].at[0, :, columns(me)], rows_ref.at[me, array], in_recv.at[array, 0]
+        )
+
+    def outbound(array, distance, origin):
+        return pltpu.make_async_remote_copy(
+            src_ref=out_ref.at[before(distance), array],
+            dst_ref=results[array].at[0, :, columns(origin)],
+            send_sem=out_send.at[array, distance],
+            recv_sem=out_recv.at[array, distance],
+            device_id={"seq": before(distance)},
+            device_id_type=pl.DeviceIdType.MESH,
+        )
+
+    def outbound_own(array):
+        return pltpu.make_async_copy(
+            out_ref.at[me, array], results[array].at[0, :, columns(me)], out_recv.at[array, 0]
+        )
+
+    for arrays in ((1,), (2,), (0, 3)):
+        for array in arrays:
+            inbound_own(array).start()
+
+        def send(distance, carry, arrays=arrays):
+            for array in arrays:
+                inbound(array, distance, me).start()
+            return carry
+
+        lax.fori_loop(1, ring, send, 0)
+
+    conv_here[...] = conv_ref[:, columns(me)]
+
+    def arrived(array, distance):
+        @pl.when(distance == 0)
+        def _():
+            inbound_own(array).wait()
+
+        @pl.when(distance > 0)
+        def _():
+            inbound(array, distance, before(distance)).wait_recv()
+
+    def leave(array, distance):
+        @pl.when(distance == 0)
+        def _():
+            outbound_own(array).start()
+
+        @pl.when(distance > 0)
+        def _():
+            outbound(array, distance, me).start()
+
+    def taker(array):
+        def take_rows(distance):
+            arrived(array, distance)
+            return before(distance), rows_ref[before(distance), array]
+
+        return take_rows
 
     def key_weight(row):
-        return conv_ref[row : row + 1]
+        return conv_here[row : row + 1]
 
     def value_weight(row):
-        return conv_ref[taps + row : taps + row + 1]
+        return conv_here[taps + row : taps + row + 1]
 
     shape = (bases, blocks, levels)
-    build_levels(lambda pair: rows_ref[pair, 1], key_weight, *shape, key_wide, key_low, key_turned)
-    build_levels(
-        lambda pair: rows_ref[pair, 2], value_weight, *shape, value_wide, value_low, value_turned
-    )
     key_grad[...] = jnp.zeros_like(key_grad)
     value_grad[...] = jnp.zeros_like(value_grad)
-
-    def step(pair, carry):
+    build_levels(taker(1), key_weight, *shape, key_wide, key_low, key_turned)
+    build_levels(taker(2), value_weight, *shape, value_wide, value_low, value_turned)
+
+    def step(distance, carry):
+        pair = before(distance)
+        arrived(0, distance)
+        arrived(3, distance)
         attended, grad_q = attend_pair(
             pair,
             rows_ref[pair, 0],
@@ -563,26 +683,82 @@
         )
         out_ref[pair, 0] = attended
         out_ref[pair, 1] = grad_q
+        leave(0, distance)
+        leave(1, distance)
         return carry
 
-    lax.fori_loop(0, pairs, step, 0)
+    lax.fori_loop(0, ring, step, 0)
 
     def put_key(row, value):
-        conv_grad_ref[row : row + 1] = value * scale
+        conv_total[row : row + 1] = value * scale
 
     def put_value(row, value):
-        conv_grad_ref[taps + row : taps + row + 1] = value
+        conv_total[taps + row : taps + row + 1] = value
+
+    def finisher(array, grad_ref, factor):
+        def finish(distance, carry):
+            pair = before(distance)
+            rows = pl.ds(pl.multiple_of((1 + 2 * pair) * BLOCK, BLOCK), 2 * BLOCK)
+            out_ref[pair, array] = (grad_ref[rows] * factor).astype(jnp.bfloat16)
+            leave(array, distance)
+            return carry
+
+        return finish
 
     coarsen_gradients(key_weight, *shape, key_wide, key_grad, put_key)
+    lax.fori_loop(0, ring, finisher(2, key_grad, scale), 0)
     coarsen_gradients(value_weight, *shape, value_wide, value_grad, put_value)
 
-    def finish(pair, carry):
-        rows = pl.ds(pl.multiple_of((1 + 2 * pair) * BLOCK, BLOCK), 2 * BLOCK)
-        out_ref[pair, 2] = (key_grad[rows] * scale).astype(jnp.bfloat16)
-        out_ref[pair, 3] = value_grad[rows].astype(jnp.bfloat16)
+    def part(distance, slot):
+        other = lax.rem(group + distance, groups)
+        return pltpu.make_async_remote_copy(
+            src_ref=conv_parts.at[group],
+            dst_ref=conv_parts.at[slot],
+            send_sem=part_send.at[distance],
+            recv_sem=part_recv.at[distance],
+            device_id={"dp": other},
+            device_id_type=pl.DeviceIdType.MESH,
+        )
+
+    def gathered(distance, head):
+        return pltpu.make_async_remote_copy(
+            src_ref=conv_total,
+            dst_ref=conv_grad_ref.at[:, columns(head)],
+            send_sem=total_send.at[distance],
+            recv_sem=total_recv.at[distance],
+            device_id={"seq": after(distance)},
+            device_id_type=pl.DeviceIdType.MESH,
+        )
+
+    conv_parts[group] = conv_total[...]
+    for distance in range(1, groups):
+        part(distance, group).start()
+    lax.fori_loop(0, ring, finisher(3, value_grad, 1.0), 0)
+    for distance in range(1, groups):
+        part(distance, lax.rem(group + groups - distance, groups)).wait_recv()
+    conv_sum = conv_parts[0]
+    for slot in range(1, groups):
+        conv_sum = conv_sum + conv_parts[slot]
+    conv_total[...] = conv_sum
+    conv_grad_ref[:, columns(me)] = conv_sum
+    for distance in range(1, ring):
+        gathered(distance, me).start()
+
+    for array in range(4):
+        outbound_own(array).wait()
+
+    def settle(distance, carry):
+        for array in range(4):
+            inbound(array, distance, me).wait_send()
+            outbound(array, distance, me).wait_send()
+            outbound(array, distance, after(distance)).wait_recv()
+        gathered(distance, me).wait_send()
+        gathered(distance, before(distance)).wait_recv()
         return carry
 
-    lax.fori_loop(0, pairs, finish, 0)
+    lax.fori_loop(1, ring, settle, 0)
+    for distance in range(1, groups):
+        part(distance, group).wait_send()
 
 
 def stack_scratch(blocks, levels):
@@ -592,40 +768,41 @@
     return [flat, low, low, flat]
 
 
-def one_head(rows, conv, levels):
-    pairs = rows.shape[0]
-    pieces = 4 + 2 * levels
-    scores = pltpu.VMEM((pieces, BLOCK, 2 * BLOCK), jnp.float32)
-    return pl.pallas_call(
-        functools.partial(head_kernel, levels),
-        out_shape=(
-            jax.ShapeDtypeStruct(rows.shape, jnp.bfloat16),
-            jax.ShapeDtypeStruct(conv.shape, jnp.float32),
+def per_device_heads(queries, key_rows, value_rows, conv_key, conv_value, grad_out):
+    tok_rows, feat_width = queries.shape[1:]
+    levels = conv_key.shape[0]
+    ring, groups = lax.axis_size("seq"), lax.axis_size("dp")
+    conv = jnp.concatenate([conv_key, conv_value], 0).reshape(8 * levels, feat_width)
+    like = jax.ShapeDtypeStruct(queries.shape, jnp.bfloat16)
+    scores = pltpu.VMEM((4 + 2 * levels, BLOCK, 2 * BLOCK), jnp.float32)
+    rows = pltpu.VMEM((ring, 4, tok_rows, HEAD_DIM), jnp.bfloat16)
+    small = pltpu.VMEM((8 * levels, HEAD_DIM), jnp.float32)
+    dma = pltpu.SemaphoreType.DMA
+    anywhere = pl.BlockSpec(memory_space=pl.ANY)
+    in_vmem = pl.BlockSpec(memory_space=pltpu.VMEM)
+    outs = pl.pallas_call(
+        functools.partial(head_kernel, levels, ring, groups),
+        out_shape=(like, like, like, like, jax.ShapeDtypeStruct(conv.shape, jnp.float32)),
+        in_specs=[anywhere] * 4 + [in_vmem],
+        out_specs=[anywhere] * 4 + [in_vmem],
+        scratch_shapes=[
+            rows,
+            rows,
+            small,
+            pltpu.VMEM((groups, 8 * levels, HEAD_DIM), jnp.float32),
+            small,
+        ]
+        + stack_scratch(2 * ring, levels) * 2
+        + [scores, scores]
+        + [dma((4, ring))] * 4
+        + [dma((groups,))] * 2
+        + [dma((ring,))] * 2,
+        compiler_params=pltpu.CompilerParams(
+            collective_id=0, has_side_effects=True, vmem_limit_bytes=48 * 2**20
         ),
-        in_specs=[pl.BlockSpec(memory_space=pltpu.VMEM)] * 2,
-        out_specs=[pl.BlockSpec(memory_space=pltpu.VMEM)] * 2,
-        scratch_shapes=stack_scratch(2 * pairs, levels) * 2 + [scores, scores],
-        compiler_params=pltpu.CompilerParams(vmem_limit_bytes=48 * 2**20),
-    )(rows, conv)
-
-
-def per_device_heads(queries, key_rows, value_rows, conv_key, conv_value, grad_out):
-    tok_rows = queries.shape[1]
-    levels = conv_key.shape[0]
-    head = lax.axis_index("seq")
-    stacked = jnp.stack([queries[0], key_rows[0], value_rows[0], grad_out[0]])
-    split = stacked.reshape(4, tok_rows, HEADS, HEAD_DIM).transpose(2, 0, 1, 3)
-    rows = lax.all_to_all(split, "seq", 0, 0)
-    conv = jnp.concatenate([conv_key, conv_value], 0).reshape(8 * levels, HEADS * HEAD_DIM)
-    conv_here = lax.dynamic_slice_in_dim(conv, head * HEAD_DIM, HEAD_DIM, 1)
-    outs, conv_grad = one_head(rows, conv_here, levels)
-    back = lax.all_to_all(outs, "seq", 0, 0)
-    whole = back.transpose(1, 2, 0, 3).reshape(4, 1, tok_rows, HEADS * HEAD_DIM)
-    placed = lax.dynamic_update_slice_in_dim(
-        jnp.zeros_like(conv), conv_grad, head * HEAD_DIM, 1
-    )
-    conv_sum = lax.psum(placed, ("seq", "dp")).reshape(2, levels, 4, HEADS * HEAD_DIM)
-    return (whole[0], whole[1], whole[2], whole[3], conv_sum[0], conv_sum[1])
+    )(queries, key_rows, value_rows, grad_out, conv)
+    conv_sum = outs[4].reshape(2, levels, 4, feat_width)
+    return (outs[0], outs[1], outs[2], outs[3], conv_sum[0], conv_sum[1])
 
 
 def solution(mesh):

time: 257 us -> 119 us (0.46)
  waiting for transfers between devices: 194 us -> 0 us
  Pallas kernels: 17.8 us -> 108 us
  between operations: 14.2 us -> 0.67 us
  starting transfers between devices: 11.1 us -> 0 us
  local copies, waits for them, and re-layouts: 18.3 us -> 8.65 us
    psum x1 -> x0, waiting for transfers between devices: 146 us -> none  [per_device_heads(): lax.psum(placed, ('seq', 'dp')).reshape(2, levels, 4, HEADS * HEAD_DIM)]
    pallas_call x1, Pallas kernels: 17.8 us -> 108 us  [per_device_heads(): pl.pallas_call(functools.partial(head_kernel, levels, ring, groups), out_...]
    all_to_all x2 -> x0, waiting for transfers between devices: 48.1 us -> none  [the longest x1 48.1 us: per_device_heads(): rows = lax.all_to_all(split, 'seq', 0, 0)]
    all_to_all x2 -> x0, starting transfers between devices: 11 us -> none  [the longest x1 7.38 us: per_device_heads(): rows = lax.all_to_all(split, 'seq', 0, 0)]
    slice x6 -> x1, local copies, waits for them, and re-layouts: 4.01 us -> 0.01 us  [per_device_heads(): return (outs[0], outs[1], outs[2], outs[3], conv_sum[0], conv_sum[1])]
    unnamed x22 -> x12, local copies, waits for them, and re-layouts: 10.6 us -> 7.33 us
  transfers between devices with their start and end apart: 3 -> 0, of which waited for: 2 -> 0; matrix products, arithmetic and copies ran while one was open for 1% -> 0% of each run, Pallas kernels for 0% -> 0%
where the time goes in v2:
time: 119 us; the launch traced here: 118 us
  Pallas kernels  108 us (91%)
  local copies, waits for them, and re-layouts  8.65 us (7%)
    pallas_call x1, Pallas kernels, per_device_heads(): pl.pallas_call(functools.partial(head_kernel, levels, ring, groups), out_...  108 us
    unnamed x12, local copies, waits for them, and re-layouts  7.33 us

profile of v2, /device:TPU:0, one launch (start us, length us, event | category | flops | bytes accessed | tf_op | source)
XLA Modules:
  0.0 118.3 jit_solution(15717578101924672137)
XLA Ops:
  0.6 0.8 pad_maximum_fusion
  1.5 0.0 copy-start
  1.5 1.0 copy-done
  2.6 0.0 copy-start.1
  2.6 1.0 copy-done.1
  3.6 0.0 copy-start.2
  3.6 1.0 copy-done.2
  4.7 0.0 copy-start.3
  4.7 1.0 copy-done.3
  5.7 108.2 %shard_map.109 = (bf16[1,256,1024]{2,1,0:T(8,128)(2,1)S(1)}, bf16[1,256,1024]{2,1,0:T(8,128)(2,1)S(1)}, bf16[1,256,1024]{2,1,0:T(8,128)(2,1)S(1)}, bf16[1,256,1024]{2,1,0:T(8,128)(2,1)S(1)}, f32[24,1024]{1,0:T(8,128)S(1)}) custom-call(bf16[1,256,1024]{2,1,0:T(8,128)(2,1)S(1)} %copy-done, bf16[1,256,1024]{2,1,0:T(8,128)(2,1)S(1)} %copy-done.1, ...), custom_call_target="tpu_custom_call" | custom-call | tf_op jit(solution)/shard_map/pallas_call | solution.py:783
  113.9 0.6 squeeze.7
  114.5 0.6 squeeze.6
  115.2 0.8 copy.16
  116.0 0.8 copy.17
  116.7 0.8 copy.18
  117.5 0.8 copy.19
  (2 shorter events, 0.0 us)
Async XLA Ops:
  1.5 1.0 copy-start
  2.6 1.0 copy-start.1
  3.6 1.0 copy-start.2
  4.7 1.0 copy-start.3

commit v3 on v2

--- a/solution.py
+++ b/solution.py
@@ -526,12 +526,14 @@
     key_hbm,
     value_hbm,
     do_hbm,
-    conv_ref,
+    conv_key_ref,
+    conv_value_ref,
     att_hbm,
     grad_q_hbm,
     grad_key_hbm,
     grad_value_hbm,
-    conv_grad_ref,
+    conv_key_grad,
+    conv_value_grad,
     rows_ref,
     out_ref,
     conv_here,
@@ -560,9 +562,9 @@
     group = lax.axis_index("dp")
     blocks = 2 * ring
     bases, _ = level_bases(blocks, levels)
-    taps = 4 * levels
     scale = HEAD_DIM**-0.5
     sources = (q_hbm, key_hbm, value_hbm, do_hbm)
+    conv_grads = (conv_key_grad, conv_value_grad)
     results = (att_hbm, grad_q_hbm, grad_key_hbm, grad_value_hbm)
 
     def after(distance):
@@ -618,18 +620,21 @@
             out_ref.at[me, array], results[array].at[0, :, columns(me)], out_recv.at[array, 0]
         )
 
-    for arrays in ((1,), (2,), (0, 3)):
+    def send(*arrays):
         for array in arrays:
             inbound_own(array).start()
 
-        def send(distance, carry, arrays=arrays):
+        def step(distance, carry):
             for array in arrays:
                 inbound(array, distance, me).start()
             return carry
 
-        lax.fori_loop(1, ring, send, 0)
-
-    conv_here[...] = conv_ref[:, columns(me)]
+        lax.fori_loop(1, ring, step, 0)
+
+    send(1)
+    send(2)
+    conv_here[0] = conv_key_ref[:, :, columns(me)]
+    conv_here[1] = conv_value_ref[:, :, columns(me)]
 
     def arrived(array, distance):
         @pl.when(distance == 0)
@@ -657,15 +662,16 @@
         return take_rows
 
     def key_weight(row):
-        return conv_here[row : row + 1]
+        return conv_here[0, row // 4, row % 4 : row % 4 + 1]
 
     def value_weight(row):
-        return conv_here[taps + row : taps + row + 1]
+        return conv_here[1, row // 4, row % 4 : row % 4 + 1]
 
     shape = (bases, blocks, levels)
     key_grad[...] = jnp.zeros_like(key_grad)
     value_grad[...] = jnp.zeros_like(value_grad)
     build_levels(taker(1), key_weight, *shape, key_wide, key_low, key_turned)
+    send(0, 3)
     build_levels(taker(2), value_weight, *shape, value_wide, value_low, value_turned)
 
     def step(distance, carry):
@@ -690,10 +696,10 @@
     lax.fori_loop(0, ring, step, 0)
 
     def put_key(row, value):
-        conv_total[row : row + 1] = value * scale
+        conv_total[0, row // 4, row % 4 : row % 4 + 1] = value * scale
 
     def put_value(row, value):
-        conv_total[taps + row : taps + row + 1] = value
+        conv_total[1, row // 4, row % 4 : row % 4 + 1] = value
 
     def finisher(array, grad_ref, factor):
         def finish(distance, carry):
@@ -720,12 +726,12 @@
             device_id_type=pl.DeviceIdType.MESH,
         )
 
-    def gathered(distance, head):
+    def gathered(kind, distance, head):
         return pltpu.make_async_remote_copy(
-            src_ref=conv_total,
-            dst_ref=conv_grad_ref.at[:, columns(head)],
-            send_sem=total_send.at[distance],
-            recv_sem=total_recv.at[distance],
+            src_ref=conv_total.at[kind],
+            dst_ref=conv_grads[kind].at[:, :, columns(head)],
+            send_sem=total_send.at[kind, distance],
+            recv_sem=total_recv.at[kind, distance],
             device_id={"seq": after(distance)},
             device_id_type=pl.DeviceIdType.MESH,
         )
@@ -740,9 +746,10 @@
     for slot in range(1, groups):
         conv_sum = conv_sum + conv_parts[slot]
     conv_total[...] = conv_sum
-    conv_grad_ref[:, columns(me)] = conv_sum
-    for distance in range(1, ring):
-        gathered(distance, me).start()
+    for kind in range(2):
+        conv_grads[kind][:, :, columns(me)] = conv_sum[kind]
+        for distance in range(1, ring):
+            gathered(kind, distance, me).start()
 
     for array in range(4):
         outbound_own(array).wait()
@@ -752,8 +759,9 @@
             inbound(array, distance, me).wait_send()
             outbound(array, distance, me).wait_send()
             outbound(array, distance, after(distance)).wait_recv()
-        gathered(distance, me).wait_send()
-        gathered(distance, before(distance)).wait_recv()
+        for kind in range(2):
+            gathered(kind, distance, me).wait_send()
+            gathered(kind, distance, before(distance)).wait_recv()
         return carry
 
     lax.fori_loop(1, ring, settle, 0)
@@ -769,40 +777,38 @@
 
 
 def per_device_heads(queries, key_rows, value_rows, conv_key, conv_value, grad_out):
-    tok_rows, feat_width = queries.shape[1:]
+    tok_rows = queries.shape[1]
     levels = conv_key.shape[0]
     ring, groups = lax.axis_size("seq"), lax.axis_size("dp")
-    conv = jnp.concatenate([conv_key, conv_value], 0).reshape(8 * levels, feat_width)
     like = jax.ShapeDtypeStruct(queries.shape, jnp.bfloat16)
+    conv_like = jax.ShapeDtypeStruct(conv_key.shape, jnp.float32)
     scores = pltpu.VMEM((4 + 2 * levels, BLOCK, 2 * BLOCK), jnp.float32)
     rows = pltpu.VMEM((ring, 4, tok_rows, HEAD_DIM), jnp.bfloat16)
-    small = pltpu.VMEM((8 * levels, HEAD_DIM), jnp.float32)
+    small = (2, levels, 4, HEAD_DIM)
     dma = pltpu.SemaphoreType.DMA
-    anywhere = pl.BlockSpec(memory_space=pl.ANY)
+    in_hbm = pl.BlockSpec(memory_space=pltpu.HBM)
     in_vmem = pl.BlockSpec(memory_space=pltpu.VMEM)
-    outs = pl.pallas_call(
+    return pl.pallas_call(
         functools.partial(head_kernel, levels, ring, groups),
-        out_shape=(like, like, like, like, jax.ShapeDtypeStruct(conv.shape, jnp.float32)),
-        in_specs=[anywhere] * 4 + [in_vmem],
-        out_specs=[anywhere] * 4 + [in_vmem],
+        out_shape=(like, like, like, like, conv_like, conv_like),
+        in_specs=[in_hbm] * 4 + [in_vmem] * 2,
+        out_specs=[in_hbm] * 4 + [in_vmem] * 2,
         scratch_shapes=[
             rows,
             rows,
-            small,
-            pltpu.VMEM((groups, 8 * levels, HEAD_DIM), jnp.float32),
-            small,
+            pltpu.VMEM(small, jnp.float32),
+            pltpu.VMEM((groups,) + small, jnp.float32),
+            pltpu.VMEM(small, jnp.float32),
         ]
         + stack_scratch(2 * ring, levels) * 2
         + [scores, scores]
         + [dma((4, ring))] * 4
         + [dma((groups,))] * 2
-        + [dma((ring,))] * 2,
+        + [dma((2, ring))] * 2,
         compiler_params=pltpu.CompilerParams(
-            collective_id=0, has_side_effects=True, vmem_limit_bytes=48 * 2**20
+            collective_id=0, has_side_effects=True, vmem_limit_bytes=56 * 2**20
         ),
-    )(queries, key_rows, value_rows, grad_out, conv)
-    conv_sum = outs[4].reshape(2, levels, 4, feat_width)
-    return (outs[0], outs[1], outs[2], outs[3], conv_sum[0], conv_sum[1])
+    )(queries, key_rows, value_rows, grad_out, conv_key, conv_value)
 
 
 def solution(mesh):

time: 119 us -> 118 us (level)
  local copies, waits for them, and re-layouts: 8.65 us -> 6.62 us
  Pallas kernels: 108 us -> 110 us
    pallas_call x1, Pallas kernels: 108 us -> 110 us  [per_device_heads(): pl.pallas_call(functools.partial(head_kernel, levels, ring, groups), out_...]
    squeeze x2 -> x0, local copies, waits for them, and re-layouts: 1.27 us -> none  [per_device_heads(): return (outs[0], outs[1], outs[2], outs[3], conv_sum[0], conv_sum[1])]
    unnamed x12 -> x16, local copies, waits for them, and re-layouts: 7.33 us -> 6.62 us
where the time goes in v3:
time: 118 us
  Pallas kernels  110 us (93%)
  local copies, waits for them, and re-layouts  6.62 us (6%)
    pallas_call x1, Pallas kernels, per_device_heads(): pl.pallas_call(functools.partial(head_kernel, levels, ring, groups), out_...  110 us
    unnamed x16, local copies, waits for them, and re-layouts  6.62 us

profile of v3, /device:TPU:0, one launch (start us, length us, event | category | flops | bytes accessed | tf_op | source)
XLA Modules:
  0.0 117.6 jit_solution(7251721804288105117)
XLA Ops:
  0.6 110.3 %shard_map.109 = (bf16[1,256,1024]{2,1,0:T(8,128)(2,1)}, bf16[1,256,1024]{2,1,0:T(8,128)(2,1)}, bf16[1,256,1024]{2,1,0:T(8,128)(2,1)}, bf16[1,256,1024]{2,1,0:T(...) custom-call(bf16[1,256,1024]{2,1,0:T(8,128)(2,1)} %q_hbm.1, bf16[1,256,1024]{2,1,0:T(8,128)(2,1)} %key_hbm.1, ...), custom_call_target="tpu_custom_call" | custom-call | tf_op jit(solution)/shard_map/pallas_call | solution.py:791
  111.0 0.0 copy-start.2
  111.0 1.9 %copy.18 = bf16[1,256,1024]{2,1,0:T(8,128)(2,1)} copy(bf16[1,256,1024]{2,1,0:T(8,128)(2,1)} %get-tuple-element.12) | data formatting | bytes 1048576
  112.9 0.0 copy-done.2
  112.9 0.0 copy-start.1
  112.9 0.8 copy.19
  113.7 0.4 copy-done.1
  114.1 0.0 copy-start
  114.1 0.8 copy.20
  114.9 0.4 copy-done
  115.4 0.0 copy-start.4
  115.4 0.8 copy.21
  116.2 0.0 copy-done.4
  116.2 0.0 copy-start.3
  116.2 0.6 copy.22
  116.8 0.2 copy-done.3
  117.0 0.6 copy.23
Async XLA Ops:
  111.0 1.9 %copy-start.2 = (bf16[1,256,1024]{2,1,0:T(8,128)(2,1)S(1)}, bf16[1,256,1024]{2,1,0:T(8,128)(2,1)}, u32[]{:S(2)}) copy-start(bf16[1,256,1024]{2,1,0:T(8,128)(2,1)} %get-tuple-element.13) | copy-start | bytes 1572868
  112.9 1.2 %copy-start.1 = (bf16[1,256,1024]{2,1,0:T(8,128)(2,1)S(1)}, bf16[1,256,1024]{2,1,0:T(8,128)(2,1)}, u32[]{:S(2)}) copy-start(bf16[1,256,1024]{2,1,0:T(8,128)(2,1)} %get-tuple-element.14) | copy-start | bytes 1572868
  114.1 1.2 %copy-start = (bf16[1,256,1024]{2,1,0:T(8,128)(2,1)S(1)}, bf16[1,256,1024]{2,1,0:T(8,128)(2,1)}, u32[]{:S(2)}) copy-start(bf16[1,256,1024]{2,1,0:T(8,128)(2,1)} %get-tuple-element.15) | copy-start | bytes 1572868
  115.4 0.8 copy-start.4
  116.2 0.8 copy-start.3

commit v4 on v3

--- a/solution.py
+++ b/solution.py
@@ -385,6 +385,7 @@
 
 LOG2E = 1.4426950408889634
 MASKED = -1e30
+EDGE = 16
 
 
 def level_bases(blocks, levels):
@@ -395,14 +396,18 @@
     return bases, offset
 
 
-def build_levels(take_rows, weight, bases, blocks, levels, wide_ref, low_ref, turned_ref):
+def build_levels(
+    take_rows, edge, half, weight, bases, blocks, levels, wide_ref, low_ref, turned_ref
+):
     zero_wide = jnp.zeros((BLOCK, HEAD_DIM), jnp.float32)
     zero_low = jnp.zeros((BLOCK, HEAD_DIM), jnp.bfloat16)
     for level_id in range(levels + 1):
-        for pad in (bases[level_id], bases[level_id] + (blocks >> level_id) + 1):
+        count = blocks >> level_id
+        for pad in (bases[level_id], bases[level_id] + count + 1):
             wide_ref[pad * BLOCK : (pad + 1) * BLOCK] = zero_wide
-            low_ref[pad] = zero_low
-            turned_ref[pad] = zero_low
+        outer = bases[level_id] + half * (count + 1)
+        low_ref[outer] = zero_low
+        turned_ref[outer] = zero_low
 
     def put(index, low):
         wide = low.astype(jnp.float32)
@@ -417,6 +422,15 @@
         return carry
 
     lax.fori_loop(0, blocks // 2, put_pair, 0)
+    wide_ref[BLOCK - EDGE : BLOCK] = edge.astype(jnp.float32)
+    for level_id in range(1, levels):
+        start = (bases[level_id - 1] + 1) * BLOCK - EDGE - 2
+        summed = jnp.zeros((EDGE // 2, HEAD_DIM), jnp.float32)
+        for tap in range(4):
+            row = 4 * (level_id - 1) + tap
+            summed = summed + weight(row) * wide_ref[pl.ds(start + tap, EDGE // 2, stride=2)]
+        stop = (bases[level_id] + 1) * BLOCK
+        wide_ref[stop - EDGE // 2 : stop] = summed.astype(jnp.bfloat16).astype(jnp.float32)
     for level_id in range(1, levels + 1):
         for block in range(blocks >> level_id):
             start = (bases[level_id - 1] + 1 + 2 * block) * BLOCK - 2
@@ -427,7 +441,7 @@
             put(bases[level_id] + 1 + block, summed.astype(jnp.bfloat16))
 
 
-def attend_pair(pair, q_rows, do_rows, bases, blocks, levels, keys, values, scratch):
+def attend_pair(pair, whole_pair, all_pairs, q_rows, do_rows, bases, blocks, levels, keys, values, scratch):
     key_low, key_turned, key_grad = keys
     value_low, value_turned, value_grad = values
     score_ref, dprob_ref = scratch
@@ -436,20 +450,20 @@
     q_turned = q_rows.astype(jnp.float32).T.astype(jnp.bfloat16)
     do_turned = do_rows.astype(jnp.float32).T.astype(jnp.bfloat16)
     lane = lax.broadcasted_iota(jnp.int32, (1, two), 1)
-    pairs = blocks // 2
     places = [2 * pair, 2 * pair + 1, 2 * pair + 2, 2 * pair + 3]
     spans = [
-        (0, jnp.where(pair > 0, BLOCK, 0)),
+        (0, jnp.where(whole_pair > 0, BLOCK, 0)),
         None,
         None,
-        (jnp.where(pair + 1 < pairs, BLOCK, two), two),
+        (jnp.where(whole_pair + 1 < all_pairs, BLOCK, two), two),
     ]
     for level_id in range(1, levels + 1):
         coarse_id = pair // 2 ** (level_id - 1)
+        whole_id = whole_pair // 2 ** (level_id - 1)
         places += [bases[level_id] + coarse_id, bases[level_id] + coarse_id + 2]
         spans += [
-            (0, jnp.where(coarse_id >= 1, two, 0)),
-            (0, jnp.where(coarse_id + 1 < blocks >> level_id, two, 0)),
+            (0, jnp.where(whole_id >= 1, two, 0)),
+            (0, jnp.where(whole_id + 1 < 2 * all_pairs >> level_id, two, 0)),
         ]
     row_max = jnp.full((1, two), MASKED, jnp.float32)
     for piece, place in enumerate(places):
@@ -538,7 +552,12 @@
     out_ref,
     conv_here,
     conv_parts,
-    conv_total,
+    conv_slots,
+    edge_ref,
+    halo_out,
+    halo_in,
+    chain_out,
+    chain_in,
     key_wide,
     key_low,
     key_turned,
@@ -553,6 +572,14 @@
     in_recv,
     out_send,
     out_recv,
+    edge_send,
+    edge_recv,
+    block_send,
+    block_recv,
+    halo_send,
+    halo_recv,
+    chain_send,
+    chain_recv,
     part_send,
     part_recv,
     total_send,
@@ -560,25 +587,34 @@
 ):
     me = lax.axis_index("seq")
     group = lax.axis_index("dp")
-    blocks = 2 * ring
+    size = ring // 2
+    heads = HEADS // size
+    half = me // size
+    rank = lax.rem(me, size)
+    partner = lax.rem(me + size, ring)
+    blocks = 2 * size
     bases, _ = level_bases(blocks, levels)
     scale = HEAD_DIM**-0.5
     sources = (q_hbm, key_hbm, value_hbm, do_hbm)
     conv_grads = (conv_key_grad, conv_value_grad)
     results = (att_hbm, grad_q_hbm, grad_key_hbm, grad_value_hbm)
+    lows = (key_low, value_low)
+    turned = (key_turned, value_turned)
+    grads = (key_grad, value_grad)
+    wides = (key_wide, value_wide)
 
     def after(distance):
-        return lax.rem(me + distance, ring)
+        return lax.rem(rank + distance, size)
 
     def before(distance):
-        return lax.rem(me + ring - distance, ring)
+        return lax.rem(rank + size - distance, size)
 
     barrier = pltpu.get_barrier_semaphore()
     for distance in range(1, ring):
         pl.semaphore_signal(
             barrier,
             inc=1,
-            device_id={"seq": after(distance)},
+            device_id={"seq": lax.rem(me + distance, ring)},
             device_id_type=pl.DeviceIdType.MESH,
         )
     for distance in range(1, groups):
@@ -590,189 +626,338 @@
         )
     pl.semaphore_wait(barrier, ring + groups - 2)
 
-    def inbound(array, distance, landing):
+    def to_seq(source, target, send_sem, recv_sem, device):
         return pltpu.make_async_remote_copy(
-            src_ref=sources[array].at[0, :, columns(after(distance))],
-            dst_ref=rows_ref.at[landing, array],
-            send_sem=in_send.at[array, distance],
-            recv_sem=in_recv.at[array, distance],
-            device_id={"seq": after(distance)},
+            src_ref=source,
+            dst_ref=target,
+            send_sem=send_sem,
+            recv_sem=recv_sem,
+            device_id={"seq": device},
             device_id_type=pl.DeviceIdType.MESH,
         )
 
-    def inbound_own(array):
+    def inbound(array, distance, head, landing):
+        place = (array, distance, head)
+        return to_seq(
+            sources[array].at[0, :, columns(after(distance) * heads + head)],
+            rows_ref.at[landing, array, head],
+            in_send.at[place],
+            in_recv.at[place],
+            half * size + after(distance),
+        )
+
+    def inbound_own(array, head):
         return pltpu.make_async_copy(
-            sources[array].at[0, :, columns(me)], rows_ref.at[me, array], in_recv.at[array, 0]
-        )
-
-    def outbound(array, distance, origin):
-        return pltpu.make_async_remote_copy(
-            src_ref=out_ref.at[before(distance), array],
-            dst_ref=results[array].at[0, :, columns(origin)],
-            send_sem=out_send.at[array, distance],
-            recv_sem=out_recv.at[array, distance],
-            device_id={"seq": before(distance)},
-            device_id_type=pl.DeviceIdType.MESH,
-        )
-
-    def outbound_own(array):
+            sources[array].at[0, :, columns(rank * heads + head)],
+            rows_ref.at[rank, array, head],
+            in_recv.at[array, 0, head],
+        )
+
+    def outbound(array, distance, head, origin):
+        place = (array, distance, head)
+        return to_seq(
+            out_ref.at[before(distance), array, head],
+            results[array].at[0, :, columns(origin * heads + head)],
+            out_send.at[place],
+            out_recv.at[place],
+            half * size + before(distance),
+        )
+
+    def outbound_own(array, head):
         return pltpu.make_async_copy(
-            out_ref.at[me, array], results[array].at[0, :, columns(me)], out_recv.at[array, 0]
-        )
+            out_ref.at[rank, array, head],
+            results[array].at[0, :, columns(rank * heads + head)],
+            out_recv.at[array, 0, head],
+        )
+
+    def edge_copy(kind, head, other):
+        return to_seq(
+            sources[1 + kind].at[0, pl.ds(2 * BLOCK - EDGE, EDGE), columns(other * heads + head)],
+            edge_ref.at[kind, head],
+            edge_send.at[kind, head, other],
+            edge_recv.at[kind, head],
+            size + other,
+        )
+
+    def edge_place(level_id):
+        count = blocks >> level_id
+        return bases[level_id] + count - half * (count - 1)
+
+    def pad_place(level_id, of_half):
+        return bases[level_id] + (1 - of_half) * ((blocks >> level_id) + 1)
+
+    def block_copy(kind, level_id, head, pad):
+        place = (kind, level_id, head)
+        return to_seq(
+            lows[kind].at[head, edge_place(level_id)],
+            lows[kind].at[head, pad],
+            block_send.at[place],
+            block_recv.at[place],
+            partner,
+        )
+
+    def halo_copy(kind, level_id, head):
+        place = (kind, level_id, head)
+        return to_seq(
+            halo_out.at[place], halo_in.at[place], halo_send.at[place], halo_recv.at[place], partner
+        )
+
+    def chain_copy(kind, head):
+        return to_seq(
+            chain_out.at[kind, head],
+            chain_in.at[kind, head],
+            chain_send.at[kind, head],
+            chain_recv.at[kind, head],
+            partner,
+        )
+
+    every = [(kind, head) for kind in range(2) for head in range(heads)]
+
+    @pl.when(me == size - 1)
+    def _():
+        for kind, head in every:
+            for other in range(size):
+                edge_copy(kind, head, other).start()
+
+    @pl.when(half == 0)
+    def _():
+        edge_ref[...] = jnp.zeros_like(edge_ref)
 
     def send(*arrays):
         for array in arrays:
-            inbound_own(array).start()
+            for head in range(heads):
+                inbound_own(array, head).start()
 
         def step(distance, carry):
             for array in arrays:
-                inbound(array, distance, me).start()
+                for head in range(heads):
+                    inbound(array, distance, head, rank).start()
             return carry
 
-        lax.fori_loop(1, ring, step, 0)
+        lax.fori_loop(1, size, step, 0)
 
     send(1)
     send(2)
-    conv_here[0] = conv_key_ref[:, :, columns(me)]
-    conv_here[1] = conv_value_ref[:, :, columns(me)]
-
-    def arrived(array, distance):
+    for head in range(heads):
+        conv_here[0, head] = conv_key_ref[:, :, columns(rank * heads + head)]
+        conv_here[1, head] = conv_value_ref[:, :, columns(rank * heads + head)]
+
+    def arrived(array, distance, head):
         @pl.when(distance == 0)
         def _():
-            inbound_own(array).wait()
+            inbound_own(array, head).wait()
 
         @pl.when(distance > 0)
         def _():
-            inbound(array, distance, before(distance)).wait_recv()
-
-    def leave(array, distance):
+            inbound(array, distance, head, before(distance)).wait_recv()
+
+    def leave(array, distance, head):
         @pl.when(distance == 0)
         def _():
-            outbound_own(array).start()
+            outbound_own(array, head).start()
 
         @pl.when(distance > 0)
         def _():
-            outbound(array, distance, me).start()
-
-    def taker(array):
+            outbound(array, distance, head, rank).start()
+
+    def taker(array, head):
         def take_rows(distance):
-            arrived(array, distance)
-            return before(distance), rows_ref[before(distance), array]
+            arrived(array, distance, head)
+            return before(distance), rows_ref[before(distance), array, head]
 
         return take_rows
 
-    def key_weight(row):
-        return conv_here[0, row // 4, row % 4 : row % 4 + 1]
-
-    def value_weight(row):
-        return conv_here[1, row // 4, row % 4 : row % 4 + 1]
+    def weight_of(kind, head):
+        def weight(row):
+            return conv_here[kind, head, row // 4, row % 4 : row % 4 + 1]
+
+        return weight
 
     shape = (bases, blocks, levels)
     key_grad[...] = jnp.zeros_like(key_grad)
     value_grad[...] = jnp.zeros_like(value_grad)
-    build_levels(taker(1), key_weight, *shape, key_wide, key_low, key_turned)
-    send(0, 3)
-    build_levels(taker(2), value_weight, *shape, value_wide, value_low, value_turned)
-
-    def step(distance, carry):
-        pair = before(distance)
-        arrived(0, distance)
-        arrived(3, distance)
+
+    @pl.when(half == 1)
+    def _():
+        for kind, head in every:
+            edge_copy(kind, head, rank).wait_recv()
+
+    for kind in range(2):
+        for head in range(heads):
+            build_levels(
+                taker(1 + kind, head),
+                edge_ref[kind, head],
+                half,
+                weight_of(kind, head),
+                *shape,
+                wides[kind].at[head],
+                lows[kind].at[head],
+                turned[kind].at[head],
+            )
+            for level_id in range(levels, -1, -1):
+                block_copy(kind, level_id, head, pad_place(level_id, 1 - half)).start()
+        if kind == 0:
+            send(0, 3)
+    for kind, head in every:
+        for level_id in range(levels, -1, -1):
+            pad = pad_place(level_id, half)
+            block_copy(kind, level_id, head, pad).wait_recv()
+            wide = lows[kind][head, pad].astype(jnp.float32)
+            turned[kind][head, pad] = wide.T.astype(jnp.bfloat16)
+
+    def step(index, carry):
+        count = index // heads
+        head = lax.rem(index, heads)
+        pair = (1 - half) * (size - 1 - count) + half * count
+        distance = lax.rem(rank + size - pair, size)
+        arrived(0, distance, head)
+        arrived(3, distance, head)
         attended, grad_q = attend_pair(
             pair,
-            rows_ref[pair, 0],
-            rows_ref[pair, 3],
+            half * size + pair,
+            ring,
+            rows_ref[pair, 0, head],
+            rows_ref[pair, 3, head],
             *shape,
-            (key_low, key_turned, key_grad),
-            (value_low, value_turned, value_grad),
+            (key_low.at[head], key_turned.at[head], key_grad.at[head]),
+            (value_low.at[head], value_turned.at[head], value_grad.at[head]),
             (score_ref, dprob_ref),
         )
-        out_ref[pair, 0] = attended
-        out_ref[pair, 1] = grad_q
-        leave(0, distance)
-        leave(1, distance)
+        out_ref[pair, 0, head] = attended
+        out_ref[pair, 1, head] = grad_q
+        leave(0, distance, head)
+        leave(1, distance, head)
+        for level_id in range(levels + 1):
+
+            @pl.when(count == max(1, 1 << level_id >> 1) - 1)
+            def _(level_id=level_id):
+                start = pl.multiple_of(pad_place(level_id, half) * BLOCK, BLOCK)
+                for kind in range(2):
+                    rows = grads[kind][head, pl.ds(start, BLOCK)]
+                    halo_out[kind, level_id, head] = rows.astype(jnp.bfloat16)
+                    halo_copy(kind, level_id, head).start()
+
         return carry
 
-    lax.fori_loop(0, ring, step, 0)
-
-    def put_key(row, value):
-        conv_total[0, row // 4, row % 4 : row % 4 + 1] = value * scale
-
-    def put_value(row, value):
-        conv_total[1, row // 4, row % 4 : row % 4 + 1] = value
-
-    def finisher(array, grad_ref, factor):
+    lax.fori_loop(0, size * heads, step, 0)
+
+    for kind, head in every:
+        for level_id in range(levels + 1):
+            halo_copy(kind, level_id, head).wait_recv()
+            rows = pl.ds(pl.multiple_of(edge_place(level_id) * BLOCK, BLOCK), BLOCK)
+            grads[kind][head, rows] += halo_in[kind, level_id, head].astype(jnp.float32)
+
+    def finisher(array, head, grad_ref, factor):
         def finish(distance, carry):
             pair = before(distance)
             rows = pl.ds(pl.multiple_of((1 + 2 * pair) * BLOCK, BLOCK), 2 * BLOCK)
-            out_ref[pair, array] = (grad_ref[rows] * factor).astype(jnp.bfloat16)
-            leave(array, distance)
+            out_ref[pair, array, head] = (grad_ref[head, rows] * factor).astype(jnp.bfloat16)
+            leave(array, distance, head)
             return carry
 
         return finish
 
-    coarsen_gradients(key_weight, *shape, key_wide, key_grad, put_key)
-    lax.fori_loop(0, ring, finisher(2, key_grad, scale), 0)
-    coarsen_gradients(value_weight, *shape, value_wide, value_grad, put_value)
+    for kind, head in every:
+        grad_ref = grads[kind].at[head]
+
+        @pl.when(half == 0)
+        def _(kind=kind, head=head, grad_ref=grad_ref):
+            chain_copy(kind, head).wait_recv()
+            for level_id in range(1, levels + 1):
+                start = (bases[level_id] + (blocks >> level_id) + 1) * BLOCK
+                grad_ref[start : start + 8] = chain_in[kind, head, level_id - 1]
+
+        def put(row, value, kind=kind, head=head):
+            factor = 1.0 if kind else scale
+            here = slice(head * HEAD_DIM, (head + 1) * HEAD_DIM)
+            conv_parts[group, kind, row // 4, row % 4 : row % 4 + 1, here] = value * factor
+
+        coarsen_gradients(weight_of(kind, head), *shape, wides[kind].at[head], grad_ref, put)
+
+        @pl.when(half == 1)
+        def _(kind=kind, head=head, grad_ref=grad_ref):
+            for level_id in range(1, levels + 1):
+                start = (bases[level_id] + 1) * BLOCK
+                chain_out[kind, head, level_id - 1] = grad_ref[start : start + 8]
+            chain_copy(kind, head).start()
+
+        lax.fori_loop(0, size, finisher(2 + kind, head, grads[kind], 1.0 if kind else scale), 0)
 
     def part(distance, slot):
-        other = lax.rem(group + distance, groups)
         return pltpu.make_async_remote_copy(
             src_ref=conv_parts.at[group],
             dst_ref=conv_parts.at[slot],
             send_sem=part_send.at[distance],
             recv_sem=part_recv.at[distance],
-            device_id={"dp": other},
+            device_id={"dp": lax.rem(group + distance, groups)},
             device_id_type=pl.DeviceIdType.MESH,
         )
 
-    def gathered(kind, distance, head):
-        return pltpu.make_async_remote_copy(
-            src_ref=conv_total.at[kind],
-            dst_ref=conv_grads[kind].at[:, :, columns(head)],
-            send_sem=total_send.at[kind, distance],
-            recv_sem=total_recv.at[kind, distance],
-            device_id={"seq": after(distance)},
-            device_id_type=pl.DeviceIdType.MESH,
-        )
-
-    conv_parts[group] = conv_total[...]
+    def gathered(distance, slot):
+        return to_seq(
+            conv_slots.at[me],
+            conv_slots.at[slot],
+            total_send.at[distance],
+            total_recv.at[distance],
+            lax.rem(me + distance, ring),
+        )
+
     for distance in range(1, groups):
         part(distance, group).start()
-    lax.fori_loop(0, ring, finisher(3, value_grad, 1.0), 0)
     for distance in range(1, groups):
         part(distance, lax.rem(group + groups - distance, groups)).wait_recv()
     conv_sum = conv_parts[0]
     for slot in range(1, groups):
         conv_sum = conv_sum + conv_parts[slot]
-    conv_total[...] = conv_sum
+    conv_slots[me] = conv_sum
+    for distance in range(1, ring):
+        gathered(distance, me).start()
+    for distance in range(1, ring):
+        gathered(distance, lax.rem(me + ring - distance, ring)).wait_recv()
+    width = heads * HEAD_DIM
     for kind in range(2):
-        conv_grads[kind][:, :, columns(me)] = conv_sum[kind]
-        for distance in range(1, ring):
-            gathered(kind, distance, me).start()
+        for slot in range(size):
+            both = conv_slots[slot, kind] + conv_slots[size + slot, kind]
+            conv_grads[kind][:, :, slot * width : (slot + 1) * width] = both
 
     for array in range(4):
-        outbound_own(array).wait()
+        for head in range(heads):
+            outbound_own(array, head).wait()
 
     def settle(distance, carry):
         for array in range(4):
-            inbound(array, distance, me).wait_send()
-            outbound(array, distance, me).wait_send()
-            outbound(array, distance, after(distance)).wait_recv()
-        for kind in range(2):
-            gathered(kind, distance, me).wait_send()
-            gathered(kind, distance, before(distance)).wait_recv()
+            for head in range(heads):
+                inbound(array, distance, head, rank).wait_send()
+                outbound(array, distance, head, rank).wait_send()
+                outbound(array, distance, head, after(distance)).wait_recv()
         return carry
 
-    lax.fori_loop(1, ring, settle, 0)
+    lax.fori_loop(1, size, settle, 0)
+    for distance in range(1, ring):
+        gathered(distance, me).wait_send()
     for distance in range(1, groups):
         part(distance, group).wait_send()
-
-
-def stack_scratch(blocks, levels):
+    for kind, head in every:
+        for level_id in range(levels + 1):
+            block_copy(kind, level_id, head, pad_place(level_id, 1 - half)).wait_send()
+            halo_copy(kind, level_id, head).wait_send()
+
+    @pl.when(half == 1)
+    def _():
+        for kind, head in every:
+            chain_copy(kind, head).wait_send()
+
+    @pl.when(me == size - 1)
+    def _():
+        for kind, head in every:
+            for other in range(size):
+                edge_copy(kind, head, other).wait_send()
+
+
+def stack_scratch(heads, blocks, levels):
     total = level_bases(blocks, levels)[1]
-    flat = pltpu.VMEM((total * BLOCK, HEAD_DIM), jnp.float32)
-    low = pltpu.VMEM((total, BLOCK, HEAD_DIM), jnp.bfloat16)
+    flat = pltpu.VMEM((heads, total * BLOCK, HEAD_DIM), jnp.float32)
+    low = pltpu.VMEM((heads, total, BLOCK, HEAD_DIM), jnp.bfloat16)
     return [flat, low, low, flat]
 
 
@@ -780,33 +965,46 @@
     tok_rows = queries.shape[1]
     levels = conv_key.shape[0]
     ring, groups = lax.axis_size("seq"), lax.axis_size("dp")
+    size = ring // 2
+    heads = HEADS // size
     like = jax.ShapeDtypeStruct(queries.shape, jnp.bfloat16)
     conv_like = jax.ShapeDtypeStruct(conv_key.shape, jnp.float32)
     scores = pltpu.VMEM((4 + 2 * levels, BLOCK, 2 * BLOCK), jnp.float32)
-    rows = pltpu.VMEM((ring, 4, tok_rows, HEAD_DIM), jnp.bfloat16)
-    small = (2, levels, 4, HEAD_DIM)
+    rows = pltpu.VMEM((size, 4, heads, tok_rows, HEAD_DIM), jnp.bfloat16)
+    conv_part = (2, levels, 4, heads * HEAD_DIM)
+    halo = pltpu.VMEM((2, levels + 1, heads, BLOCK, HEAD_DIM), jnp.bfloat16)
+    chain = pltpu.VMEM((2, heads, levels, 8, HEAD_DIM), jnp.float32)
     dma = pltpu.SemaphoreType.DMA
     in_hbm = pl.BlockSpec(memory_space=pltpu.HBM)
+    anywhere = pl.BlockSpec(memory_space=pl.ANY)
     in_vmem = pl.BlockSpec(memory_space=pltpu.VMEM)
     return pl.pallas_call(
         functools.partial(head_kernel, levels, ring, groups),
         out_shape=(like, like, like, like, conv_like, conv_like),
         in_specs=[in_hbm] * 4 + [in_vmem] * 2,
-        out_specs=[in_hbm] * 4 + [in_vmem] * 2,
+        out_specs=[anywhere] * 4 + [in_vmem] * 2,
         scratch_shapes=[
             rows,
             rows,
-            pltpu.VMEM(small, jnp.float32),
-            pltpu.VMEM((groups,) + small, jnp.float32),
-            pltpu.VMEM(small, jnp.float32),
+            pltpu.VMEM((2, heads, levels, 4, HEAD_DIM), jnp.float32),
+            pltpu.VMEM((groups,) + conv_part, jnp.float32),
+            pltpu.VMEM((ring,) + conv_part, jnp.float32),
+            pltpu.VMEM((2, heads, EDGE, HEAD_DIM), jnp.bfloat16),
+            halo,
+            halo,
+            chain,
+            chain,
         ]
-        + stack_scratch(2 * ring, levels) * 2
+        + stack_scratch(heads, 2 * size, levels) * 2
         + [scores, scores]
-        + [dma((4, ring))] * 4
+        + [dma((4, size, heads))] * 4
+        + [dma((2, heads, size)), dma((2, heads))]
+        + [dma((2, levels + 1, heads))] * 4
+        + [dma((2, heads))] * 2
         + [dma((groups,))] * 2
-        + [dma((2, ring))] * 2,
+        + [dma((ring,))] * 2,
         compiler_params=pltpu.CompilerParams(
-            collective_id=0, has_side_effects=True, vmem_limit_bytes=56 * 2**20
+            collective_id=0, has_side_effects=True, vmem_limit_bytes=48 * 2**20
         ),
     )(queries, key_rows, value_rows, grad_out, conv_key, conv_value)
 
@@ -831,6 +1029,7 @@
     def chosen(*args):
         seq_devices = lax.axis_size("seq")
         fits = seq_devices == HEADS and args[0].shape[:2] == (1, 2 * BLOCK)
+        fits = fits and seq_devices >> args[3].shape[0] >= 1
         return (per_device_heads if fits else per_device)(*args)
 
     return jax.shard_map(

time: 118 us -> 100 us (0.85)
  Pallas kernels: 110 us -> 88.9 us
  local copies, waits for them, and re-layouts: 6.62 us -> 10.2 us
    pallas_call x1, Pallas kernels: 110 us -> 88.9 us  [per_device_heads(): pl.pallas_call(functools.partial(head_kernel, levels, ring, groups), out_...]
    unnamed x16 -> x18, local copies, waits for them, and re-layouts: 6.62 us -> 10.2 us
where the time goes in v4:
time: 100 us; the launch traced here: 99.7 us
  Pallas kernels  88.9 us (89%)
  local copies, waits for them, and re-layouts  10.2 us (10%)
    pallas_call x1, Pallas kernels, per_device_heads(): pl.pallas_call(functools.partial(head_kernel, levels, ring, groups), out_...  88.9 us
    unnamed x18, local copies, waits for them, and re-layouts  10.2 us

profile of v4, /device:TPU:0, one launch (start us, length us, event | category | flops | bytes accessed | tf_op | source)
XLA Modules:
  0.0 99.7 jit_solution(7826999864314127346)
XLA Ops:
  0.6 0.0 copy-start
  0.6 1.0 %copy-done = bf16[1,256,1024]{2,1,0:T(8,128)(2,1)S(1)} copy-done((bf16[1,256,1024]{2,1,0:T(8,128)(2,1)S(1)}, bf16[1,256,1024]{2,1,0:T(8,128)(2,1)}, u32[]{:S(2)}) %copy-start) | copy-done | bytes 524312
  1.7 0.0 copy-start.1
  1.7 1.0 %copy-done.1 = bf16[1,256,1024]{2,1,0:T(8,128)(2,1)S(1)} copy-done((bf16[1,256,1024]{2,1,0:T(8,128)(2,1)S(1)}, bf16[1,256,1024]{2,1,0:T(8,128)(2,1)}, u32[]{:S(2)}) %copy-start.1) | copy-done | bytes 524312
  2.7 0.0 copy-start.2
  2.7 1.0 %copy-done.2 = bf16[1,256,1024]{2,1,0:T(8,128)(2,1)S(1)} copy-done((bf16[1,256,1024]{2,1,0:T(8,128)(2,1)S(1)}, bf16[1,256,1024]{2,1,0:T(8,128)(2,1)}, u32[]{:S(2)}) %copy-start.2) | copy-done | bytes 524312
  3.8 0.0 copy-start.3
  3.8 1.0 %copy-done.3 = bf16[1,256,1024]{2,1,0:T(8,128)(2,1)S(1)} copy-done((bf16[1,256,1024]{2,1,0:T(8,128)(2,1)S(1)}, bf16[1,256,1024]{2,1,0:T(8,128)(2,1)}, u32[]{:S(2)}) %copy-start.3) | copy-done | bytes 524312
  4.8 0.0 copy-start.4
  4.8 0.8 copy-done.4
  5.6 0.0 copy-start.5
  5.6 0.8 copy-done.5
  6.4 88.9 %shard_map.109 = (bf16[1,256,1024]{2,1,0:T(8,128)(2,1)S(1)}, bf16[1,256,1024]{2,1,0:T(8,128)(2,1)S(1)}, bf16[1,256,1024]{2,1,0:T(8,128)(2,1)S(1)}, bf16[1,256,10...) custom-call(bf16[1,256,1024]{2,1,0:T(8,128)(2,1)S(1)} %copy-done, ...), custom_call_target="tpu_custom_call" | custom-call | tf_op jit(solution)/shard_map/pallas_call | solution.py:981
  95.3 0.8 copy.18
  96.1 0.8 copy.19
  96.9 0.8 copy.20
  97.7 0.8 copy.21
  98.5 0.6 copy.22
  99.1 0.6 copy.23
Async XLA Ops:
  0.6 1.0 %copy-start = (bf16[1,256,1024]{2,1,0:T(8,128)(2,1)S(1)}, bf16[1,256,1024]{2,1,0:T(8,128)(2,1)}, u32[]{:S(2)}) copy-start(bf16[1,256,1024]{2,1,0:T(8,128)(2,1)} %q_hbm.1) | copy-start | bytes 1572868
  1.7 1.0 %copy-start.1 = (bf16[1,256,1024]{2,1,0:T(8,128)(2,1)S(1)}, bf16[1,256,1024]{2,1,0:T(8,128)(2,1)}, u32[]{:S(2)}) copy-start(bf16[1,256,1024]{2,1,0:T(8,128)(2,1)} %key_hbm.1) | copy-start | bytes 1572868
  2.7 1.0 %copy-start.2 = (bf16[1,256,1024]{2,1,0:T(8,128)(2,1)S(1)}, bf16[1,256,1024]{2,1,0:T(8,128)(2,1)}, u32[]{:S(2)}) copy-start(bf16[1,256,1024]{2,1,0:T(8,128)(2,1)} %value_hbm.1) | copy-start | bytes 1572868
  3.8 1.0 %copy-start.3 = (bf16[1,256,1024]{2,1,0:T(8,128)(2,1)S(1)}, bf16[1,256,1024]{2,1,0:T(8,128)(2,1)}, u32[]{:S(2)}) copy-start(bf16[1,256,1024]{2,1,0:T(8,128)(2,1)} %do_hbm.1) | copy-start | bytes 1572868
  4.8 0.8 copy-start.4
  5.6 0.8 copy-start.5

commit v5 on v4

--- a/solution.py
+++ b/solution.py
@@ -711,7 +711,7 @@
             partner,
         )
 
-    every = [(kind, head) for kind in range(2) for head in range(heads)]
+    every = [(kind, head) for head in range(heads) for kind in range(2)]
 
     @pl.when(me == size - 1)
     def _():
@@ -723,21 +723,21 @@
     def _():
         edge_ref[...] = jnp.zeros_like(edge_ref)
 
-    def send(*arrays):
+    def send(head, *arrays):
         for array in arrays:
-            for head in range(heads):
-                inbound_own(array, head).start()
+            inbound_own(array, head).start()
 
         def step(distance, carry):
             for array in arrays:
-                for head in range(heads):
-                    inbound(array, distance, head, rank).start()
+                inbound(array, distance, head, rank).start()
             return carry
 
         lax.fori_loop(1, size, step, 0)
 
-    send(1)
-    send(2)
+    for head in range(heads):
+        send(head, 1)
+        send(head, 2)
+        send(head, 0, 3)
     for head in range(heads):
         conv_here[0, head] = conv_key_ref[:, :, columns(rank * heads + head)]
         conv_here[1, head] = conv_value_ref[:, :, columns(rank * heads + head)]
@@ -782,32 +782,33 @@
         for kind, head in every:
             edge_copy(kind, head, rank).wait_recv()
 
-    for kind in range(2):
-        for head in range(heads):
-            build_levels(
-                taker(1 + kind, head),
-                edge_ref[kind, head],
-                half,
-                weight_of(kind, head),
-                *shape,
-                wides[kind].at[head],
-                lows[kind].at[head],
-                turned[kind].at[head],
-            )
-            for level_id in range(levels, -1, -1):
-                block_copy(kind, level_id, head, pad_place(level_id, 1 - half)).start()
-        if kind == 0:
-            send(0, 3)
     for kind, head in every:
+        build_levels(
+            taker(1 + kind, head),
+            edge_ref[kind, head],
+            half,
+            weight_of(kind, head),
+            *shape,
+            wides[kind].at[head],
+            lows[kind].at[head],
+            turned[kind].at[head],
+        )
         for level_id in range(levels, -1, -1):
-            pad = pad_place(level_id, half)
-            block_copy(kind, level_id, head, pad).wait_recv()
-            wide = lows[kind][head, pad].astype(jnp.float32)
-            turned[kind][head, pad] = wide.T.astype(jnp.bfloat16)
+            block_copy(kind, level_id, head, pad_place(level_id, 1 - half)).start()
 
     def step(index, carry):
-        count = index // heads
-        head = lax.rem(index, heads)
+        head = index // size
+        count = lax.rem(index, size)
+
+        @pl.when(count == 0)
+        def _():
+            for kind in range(2):
+                for level_id in range(levels, -1, -1):
+                    pad = pad_place(level_id, half)
+                    block_copy(kind, level_id, head, pad).wait_recv()
+                    wide = lows[kind][head, pad].astype(jnp.float32)
+                    turned[kind][head, pad] = wide.T.astype(jnp.bfloat16)
+
         pair = (1 - half) * (size - 1 - count) + half * count
         distance = lax.rem(rank + size - pair, size)
         arrived(0, distance, head)
@@ -841,12 +842,6 @@
 
     lax.fori_loop(0, size * heads, step, 0)
 
-    for kind, head in every:
-        for level_id in range(levels + 1):
-            halo_copy(kind, level_id, head).wait_recv()
-            rows = pl.ds(pl.multiple_of(edge_place(level_id) * BLOCK, BLOCK), BLOCK)
-            grads[kind][head, rows] += halo_in[kind, level_id, head].astype(jnp.float32)
-
     def finisher(array, head, grad_ref, factor):
         def finish(distance, carry):
             pair = before(distance)
@@ -859,6 +854,10 @@
 
     for kind, head in every:
         grad_ref = grads[kind].at[head]
+        for level_id in range(levels + 1):
+            halo_copy(kind, level_id, head).wait_recv()
+            rows = pl.ds(pl.multiple_of(edge_place(level_id) * BLOCK, BLOCK), BLOCK)
+            grad_ref[rows] += halo_in[kind, level_id, head].astype(jnp.float32)
 
         @pl.when(half == 0)
         def _(kind=kind, head=head, grad_ref=grad_ref):
@@ -1004,7 +1003,7 @@
         + [dma((groups,))] * 2
         + [dma((ring,))] * 2,
         compiler_params=pltpu.CompilerParams(
-            collective_id=0, has_side_effects=True, vmem_limit_bytes=48 * 2**20
+            collective_id=0, has_side_effects=True, vmem_limit_bytes=56 * 2**20
         ),
     )(queries, key_rows, value_rows, grad_out, conv_key, conv_value)
 

time: 100 us -> 93.5 us (0.935)
  local copies, waits for them, and re-layouts: 10.2 us -> 6.62 us
  Pallas kernels: 88.9 us -> 85.8 us
    unnamed x18 -> x16, local copies, waits for them, and re-layouts: 10.2 us -> 6.62 us
    pallas_call x1, Pallas kernels: 88.9 us -> 85.8 us  [per_device_heads(): pl.pallas_call(functools.partial(head_kernel, levels, ring, groups), out_...]
where the time goes in v5:
time: 93.5 us; the launch traced here: 93.1 us
  Pallas kernels  85.8 us (92%)
  local copies, waits for them, and re-layouts  6.62 us (7%)
    pallas_call x1, Pallas kernels, per_device_heads(): pl.pallas_call(functools.partial(head_kernel, levels, ring, groups), out_...  85.8 us
    unnamed x16, local copies, waits for them, and re-layouts  6.62 us

profile of v5, /device:TPU:0, one launch (start us, length us, event | category | flops | bytes accessed | tf_op | source)
XLA Modules:
  0.0 93.1 jit_solution(13168290079828165356)
XLA Ops:
  0.6 85.8 %shard_map.109 = (bf16[1,256,1024]{2,1,0:T(8,128)(2,1)}, bf16[1,256,1024]{2,1,0:T(8,128)(2,1)}, bf16[1,256,1024]{2,1,0:T(8,128)(2,1)}, bf16[1,256,1024]{2,1,0:T(...) custom-call(bf16[1,256,1024]{2,1,0:T(8,128)(2,1)} %q_hbm.1, bf16[1,256,1024]{2,1,0:T(8,128)(2,1)} %key_hbm.1, ...), custom_call_target="tpu_custom_call" | custom-call | tf_op jit(solution)/shard_map/pallas_call | solution.py:980
  86.4 0.0 copy-start.2
  86.4 1.9 %copy.18 = bf16[1,256,1024]{2,1,0:T(8,128)(2,1)} copy(bf16[1,256,1024]{2,1,0:T(8,128)(2,1)} %get-tuple-element.12) | data formatting | bytes 1048576
  88.3 0.0 copy-done.2
  88.4 0.0 copy-start.1
  88.4 0.8 copy.19
  89.1 0.4 copy-done.1
  89.6 0.0 copy-start
  89.6 0.8 copy.20
  90.4 0.4 copy-done
  90.8 0.0 copy-start.4
  90.8 0.8 copy.21
  91.6 0.0 copy-done.4
  91.6 0.0 copy-start.3
  91.6 0.6 copy.22
  92.2 0.2 copy-done.3
  92.4 0.6 copy.23
Async XLA Ops:
  86.4 1.9 %copy-start.2 = (bf16[1,256,1024]{2,1,0:T(8,128)(2,1)S(1)}, bf16[1,256,1024]{2,1,0:T(8,128)(2,1)}, u32[]{:S(2)}) copy-start(bf16[1,256,1024]{2,1,0:T(8,128)(2,1)} %get-tuple-element.13) | copy-start | bytes 1572868
  88.4 1.2 %copy-start.1 = (bf16[1,256,1024]{2,1,0:T(8,128)(2,1)S(1)}, bf16[1,256,1024]{2,1,0:T(8,128)(2,1)}, u32[]{:S(2)}) copy-start(bf16[1,256,1024]{2,1,0:T(8,128)(2,1)} %get-tuple-element.14) | copy-start | bytes 1572868
  89.6 1.2 %copy-start = (bf16[1,256,1024]{2,1,0:T(8,128)(2,1)S(1)}, bf16[1,256,1024]{2,1,0:T(8,128)(2,1)}, u32[]{:S(2)}) copy-start(bf16[1,256,1024]{2,1,0:T(8,128)(2,1)} %get-tuple-element.15) | copy-start | bytes 1572868
  90.8 0.8 copy-start.4
  91.6 0.8 copy-start.3
